TPU v7x, 1024 devices: a whole 4x4x32 slice. The times are simulated.
1024 devices in a mesh: table: 64 (over z, core), dp: 16 (over x, y).
Axes of the slice: x: 4, y: 4, z: 32, core: 2. Of those that a mesh axis runs over, the one named last changes fastest.
Arguments:
- emb_table: float32 [3, 16384, 256], P(None, 'table'), may hold values from -4 to 4
- row_request: int32 [64, 16, 3, 64, 8], P('table', 'dp'), may hold values from 0 to 255, as said below
- live_count: int32 [64, 16, 3, 64], P('table', 'dp'), may hold values from 4 to 8, as said below
- inverse: int32 [64, 16, 3, 2048], P('table', 'dp'), may hold values from 0 to 511, as said below
- bag_ids: int32 [64, 16, 3, 2048], P('table', 'dp'), may hold values from 0 to 511, never falling along the last dimension, each value on 1 to 8 neighbouring positions
- labels: int32 [524288], P(('table', 'dp')), may hold values 0 or 1
- w_hidden: bfloat16 [768, 512], replicated, may hold values from -0.21875 to 0.21875
- b_hidden: float32 [512], replicated, may hold values from -3 to 3
- w_out: float32 [512], replicated, may hold values from -0.25 to 0.25
Outputs:
- emb_grad: float32 [16, 3, 16384, 256], P('dp', None, 'table')
- grad_w_hidden: float32 [768, 512], replicated
- grad_b_hidden: float32 [512], replicated
- grad_w_out: float32 [512], replicated
Inputs may be any that keep to these rules, and one draw needn't show every extreme that they name: `row_request`: for each device, table and owner the 8 ids are distinct. `live_count`: for each device and table at least one owner has all 8 slots live. `inverse`: every entry p * 8 + c names a live slot: c < live_count of that device, table and owner p.
All inputs are finite; a program needn't handle non-finite values. No bound on the sum of `labels` on one device may be relied on, other than what follows from the above.
Results may differ from a plain program's by a relative error of at most 0.0026.
Values sent between devices are 32-bit elements; how exact they have to be, the bound alone decides.
No kernel may reach another device: no remote copies, remote signals or barrier semaphores. Data moves between devices by JAX's collectives and lax.ppermute only.
A program may use at most 32 MiB of HBM per device.

v0:
```python
import jax
import jax.numpy as jnp
from jax import lax
from jax.sharding import PartitionSpec as P


def pick_rows(table_rows, index):
    return table_rows[index]


def scatter_rows(grad_table, index, values):
    return grad_table.at[index.reshape(-1)].add(values.reshape(-1, values.shape[-1]))


def shards(emb_table, row_request, live_count, inverse, bag_ids, labels, w_hidden, b_hidden, w_out):
    request = row_request[0, 0]
    counts = live_count[0, 0]
    slot_unique = inverse[0, 0]
    slot_sample = bag_ids[0, 0]
    num_tables, num_owners, capacity = request.shape
    row_width = emb_table.shape[2]
    samples = labels.shape[0]
    requested = lax.all_to_all(request, "table", split_axis=1, concat_axis=1, tiled=True)
    served = jax.vmap(pick_rows)(emb_table, requested)
    fetched = lax.all_to_all(served, "table", split_axis=1, concat_axis=1, tiled=True)
    slot_index = lax.broadcasted_iota(jnp.int32, (num_tables, num_owners, capacity), 2)
    live_mask = (slot_index < counts[:, :, None]).astype(jnp.float32)
    unique_rows = (fetched * live_mask[..., None]).reshape(
        num_tables, num_owners * capacity, row_width
    )
    slot_rows = jax.vmap(pick_rows)(unique_rows, slot_unique)

    def pool_slots(rows_in, segment):
        return jax.ops.segment_sum(rows_in, segment, num_segments=samples, indices_are_sorted=True)

    pooled = jax.vmap(pool_slots)(slot_rows, slot_sample)
    features = (
        jnp.transpose(pooled, (1, 0, 2))
        .reshape(samples, num_tables * row_width)
        .astype(jnp.bfloat16)
    )
    pre = jnp.dot(features, w_hidden, preferred_element_type=jnp.float32) + b_hidden
    sigma = jax.nn.sigmoid(pre)
    hidden = pre * sigma
    logit = jnp.dot(hidden, w_out, precision=lax.Precision.HIGHEST)
    error = jax.nn.sigmoid(logit) - labels.astype(jnp.float32)
    grad_pre = error[:, None] * w_out[None, :] * sigma * (1.0 + pre * (1.0 - sigma))
    grad_pre_b = grad_pre.astype(jnp.bfloat16)
    grad_features = lax.dot_general(
        grad_pre_b, w_hidden, (((1,), (1,)), ((), ())), preferred_element_type=jnp.float32
    )
    grad_tables = jnp.transpose(grad_features.reshape(samples, num_tables, row_width), (1, 0, 2))
    slot_grad = jax.vmap(pick_rows)(grad_tables, slot_sample)

    def gather_back(rows_in, segment):
        return jax.ops.segment_sum(rows_in, segment, num_segments=num_owners * capacity)

    unique_grad = jax.vmap(gather_back)(slot_grad, slot_unique).reshape(
        num_tables, num_owners, capacity, row_width
    )
    returned = lax.all_to_all(unique_grad, "table", split_axis=1, concat_axis=1, tiled=True)
    empty = jnp.zeros(emb_table.shape, jnp.float32)
    grad_shard = jax.vmap(scatter_rows)(empty, requested, returned)
    term_w = lax.dot_general(
        features, grad_pre_b, (((0,), (0,)), ((), ())), preferred_element_type=jnp.float32
    )
    term_b = jnp.sum(grad_pre, axis=0)
    term_out = jnp.dot(error, hidden, precision=lax.Precision.HIGHEST)
    sum_w, sum_b, sum_out = lax.psum((term_w, term_b, term_out), ("table", "dp"))
    total = samples * lax.axis_size("table") * lax.axis_size("dp")
    return (grad_shard[None], sum_w / total, sum_b / total, sum_out / total)


def solution(mesh):
    return jax.shard_map(
        shards,
        mesh=mesh,
        in_specs=(
            P(None, "table", None),
            P("table", "dp", None, None, None),
            P("table", "dp", None, None),
            P("table", "dp", None, None),
            P("table", "dp", None, None),
            P(("table", "dp")),
            P(),
            P(),
            P(),
        ),
        out_specs=(P("dp", None, "table", None), P(), P(), P()),
        check_vma=False,
    )
```

profile of v0, /device:TPU:1, one launch (start us, length us, event | category | flops | bytes accessed | tf_op | source)
XLA Modules:
  0.0 1378.3 jit_solution(3661557477998786877)
XLA Ops:
  7.2 0.9 copy.44
  8.1 60.9 %all_to_all.15 = s32[3,64,8]{2,0,1:T(4,128)S(1)} all-to-all(s32[3,64,8]{2,0,1:T(4,128)S(1)} %bitcast.47), channel_id=1, replica_groups=mesh['table'=64,'dp'=16] {'table'}, dimensions={1} | all-to-all | bytes 12288 | tf_op jit(solution)/shard_map/all_to_all | solution.py:23
  69.3 10.7 gather_fusion
  80.0 1.2 copy.50
  81.3 5.9 all-to-all-start.1
  88.2 151.3 %all-to-all-done.1 = f32[3,64,8,256]{3,2,0,1:T(8,128)S(1)} async-done(((f32[3,64,8,256]{3,2,0,1:T(8,128)}), f32[3,64,8,256]{3,2,0,1:T(8,128)S(1)}, u32[]{:S(2)}, u32[]{:S(2)}) %all-to-all-start.1) | async-done | bytes 1572896 | tf_op jit(solution)/shard_map/all_to_all | solution.py:25
  239.4 1.4 copy_bitcast_fusion
  240.9 79.1 %scatter_custom_fusion = f32[1536,256]{1,0:T(8,128)S(1)} fusion(s32[6144]{0:T(1024)S(1)} %reshape.156, f32[3,512,256]{2,1,0:T(8,128)} %copy_bitcast_fusion, s32[6144]{0:T(1024)S(1)} %bitcast.54, f32[]{:T(128)} %constant.6.clone.1), kind=kCustom, calls=%fused_computation.8 | custom fusion | flops 1572864 | bytes 1573376
  320.7 0.6 convolution_add_fusion
  321.3 1.2 fusion.15
  322.5 0.9 fusion.11
  323.4 1.6 copy.55
  325.0 78.0 %scatter_custom_fusion.1 = f32[1536,256]{1,0:T(8,128)S(1)} fusion(s32[6144]{0:T(1024)S(1)} %reshape.162, f32[3,512,256]{2,1,0:T(8,128)} %bitcast.41, s32[6144]{0:T(1024)S(1)} %bitcast.53, f32[]{:T(128)} %constant.6.clone.1), kind=kCustom, calls=%fused_computation.6 | custom fusion | flops 1572864 | bytes 1573376
  403.0 1.3 copy.56
  404.3 6.6 all-to-all-start.2
  411.2 3.1 fusion.9
  414.4 1.2 copy-done.3
  415.6 0.8 fusion.13
  416.8 260.4 %all-reduce = (f32[512]{0:T(512)S(1)}, f32[512]{0:T(512)S(1)}) all-reduce(f32[512]{0:T(512)S(1)} %fusion.30, f32[512]{0:T(512)S(1)} %bitcast.58), channel_id=1, replica_groups=mesh['table'=64,'dp'=16] {'table','dp'}, use_global_device_ids=true, to_apply=%region_5.0 | all-reduce | flops 1024 | bytes 8192 | tf_op jit(solution)/shard_map/psum | solution.py:69
  677.2 0.6 broadcast_multiply_fusion.2
  677.8 679.6 %all-reduce.3.cloned.1.call-done = f32[768,512]{1,0:T(8,128)} async-done(((f32[768,512]{1,0:T(8,128)}), f32[768,512]{1,0:T(8,128)}) %all-reduce.3.cloned.1.call-update) | async-done | bytes 1572880 | tf_op jit(solution)/shard_map/psum | solution.py:69
  1357.4 2.7 broadcast_multiply_fusion
  1360.1 1.3 copy.57
  1361.4 10.1 scatter_custom_fusion.2
  (57 shorter events, 2.7 us)
Async XLA Ops:
  7.2 313.2 %copy-start = (bf16[768,512]{1,0:T(8,128)(2,1)S(1)}, bf16[768,512]{1,0:T(8,128)(2,1)}, u32[]{:S(2)}) copy-start(bf16[768,512]{1,0:T(8,128)(2,1)} %param.15) | copy-start | bytes 2359300
  7.2 62.1 %copy-start.1 = (f32[3,256,256]{2,1,0:T(8,128)S(1)}, f32[3,256,256]{2,1,0:T(8,128)}, u32[]{:S(2)}) copy-start(f32[3,256,256]{2,1,0:T(8,128)} %param.9) | copy-start | bytes 2359300
  81.3 5.9 copy-start.8
  81.3 6.0 copy-start.4
  81.3 6.0 copy-start.5
  81.3 6.0 copy-start.9
  81.3 6.3 copy-start.10
  81.3 158.1 %all-to-all-start.1 = ((f32[3,64,8,256]{3,2,0,1:T(8,128)}), f32[3,64,8,256]{3,2,0,1:T(8,128)S(1)}, u32[]{:S(2)}, u32[]{:S(2)}) async-start(f32[3,64,8,256]{3,2,0,1:T(8,128)} %copy.50), calls=%async_computation.1 | async-start | bytes 3145728 | tf_op jit(solution)/shard_map/all_to_all | solution.py:25
  320.0 0.7 copy-start.13
  320.4 0.9 copy-start.6
  321.3 1.3 copy-start.2
  321.3 1.2 copy-start.7
  404.2 6.8 copy-start.12
  404.3 6.9 copy-start.11
  404.3 955.8 %all-to-all-start.2 = ((f32[3,64,8,256]{3,2,0,1:T(8,128)}), f32[3,64,8,256]{3,2,0,1:T(8,128)S(1)}, u32[]{:S(2)}, u32[]{:S(2)}) async-start(f32[3,64,8,256]{3,2,0,1:T(8,128)} %copy.56), calls=%async_computation.2 | async-start | bytes 3145728 | tf_op jit(solution)/shard_map/all_to_all | solution.py:61
  410.8 946.5 %all-reduce.3.cloned.1.call-start = ((), (), s32[]{:S(2)}) async-start(), calls=%async_computation.3 | async-start | bytes 3145728 | tf_op jit(solution)/shard_map/psum | solution.py:69
  414.3 1.2 copy-start.3
Sparse Core Ops, SparseCore 0:
  417.7 939.6 all-reduce.2
where the time goes:
time: 1380 us
  waiting for transfers between devices  831 us (60%)
  blocking collectives  321 us (23%)
  other arithmetic  173 us (13%)
  local copies, waits for them, and re-layouts  19.4 us (1%)
  between operations  14.4 us (1%)
    psum x1, waiting for transfers between devices, shards(): lax.psum((term_w, term_b, term_out), ('table', 'dp'))  680 us
    psum x1, blocking collectives, shards(): lax.psum((term_w, term_b, term_out), ('table', 'dp'))  260 us
    unnamed x10, other arithmetic  168 us
    all_to_all x1, waiting for transfers between devices, shards(): lax.all_to_all(served, 'table', split_axis=1, concat_axis=1, tiled=True)  151 us
    all_to_all x1, blocking collectives, shards(): lax.all_to_all(request, 'table', split_axis=1, concat_axis=1, tiled=True)  60.9 us
  transfers between devices with their start and end apart: 3, of which 2 were waited for; matrix products, arithmetic and copies ran while one was open for 1% of the time, Pallas kernels for 0%

commit v1 on v0

v1 whole, which is shorter than its diff:
```python
import jax
import jax.numpy as jnp
from jax import lax
from jax.experimental import pallas as pl
from jax.experimental.pallas import tpu as pltpu
from jax.sharding import Mesh, PartitionSpec as P

F32 = jnp.float32
BF16 = jnp.bfloat16
LANES = 128
TABLES = 3
ROWS_DEV = 256
WIDTH = 256
CAP = 8
N_FAR = 4
N_MID = 4
N_NEAR = 2
N_CORE = 2
N_DP = 16
N_Z = N_FAR * N_MID * N_NEAR
N_HELD = N_FAR * N_MID
N_TABLE = N_Z * N_CORE
LAYER = N_CORE * N_DP
GROUP = N_NEAR * LAYER
REQUEST_ROWS = 8
SLICE = WIDTH // N_DP
PACK = LANES // SLICE
BLOCKS = N_HELD // PACK
SAMPLES = 512
SLOTS = 2048
UNIQUE = N_TABLE * CAP
HIDDEN = 512
FEATURES = TABLES * WIDTH
TOKENS = SAMPLES * N_TABLE * N_DP
LANE_BLOCKS = HIDDEN // LANES
PIECE = FEATURES // LAYER
PIECE_ROWS = PIECE * LANE_BLOCKS
SUM_ROWS = PIECE_ROWS + 8
FAR = ("far1", "far0")
MID = ("mid1", "mid0")
COLUMN = (*FAR, *MID, "near", "core")
DP = ("x1", "x0", "y1", "y0")
SERVERS = ("near", "core", *DP)
SUMMERS = ("core", "y0", "x0", "y1", "x1")
CHUNK = 32
VMEM = 56 * 1024 * 1024


def params():
    return pltpu.CompilerParams(vmem_limit_bytes=VMEM)


def two_parts(x):
    high = x.astype(BF16)
    return high, (x - high.astype(F32)).astype(BF16)


def dot(a, b, dims=((1,), (0,))):
    return lax.dot_general(a, b, (dims, ((), ())), preferred_element_type=F32)


def slice_kernel(dp_ref, table_ref, request_ref, after_ref, out_ref, turned):
    dp = dp_ref[0]
    half = pl.multiple_of(dp // PACK * LANES, LANES)
    first = pl.multiple_of(dp % PACK * SLICE, SLICE)
    for t in range(TABLES):
        turned[...] = table_ref[t, :, pl.ds(half, LANES)].T
        out_ref[t * SLICE : (t + 1) * SLICE] = turned[pl.ds(first, SLICE), :]
    out_ref[TABLES * SLICE :] = request_ref[...]


def slice_rows(dp, emb_table, requests, after):
    whole = pl.BlockSpec(memory_space=pltpu.VMEM)
    return pl.pallas_call(
        slice_kernel,
        out_shape=jax.ShapeDtypeStruct((TABLES * SLICE + REQUEST_ROWS, ROWS_DEV), F32),
        in_specs=[pl.BlockSpec(memory_space=pltpu.SMEM), whole, whole, pl.BlockSpec(memory_space=pl.ANY)],
        out_specs=whole,
        scratch_shapes=[pltpu.VMEM((LANES, ROWS_DEV), F32)],
        compiler_params=params(),
        name="slice_rows",
    )(dp, emb_table, requests, after)


def serve_kernel(me_ref, ids_ref, slab_ref, out_ref):
    asked = GROUP * CAP
    ids = ids_ref[:, 0].reshape(asked, N_HELD)
    row = lax.broadcasted_iota(jnp.int32, (asked, ROWS_DEV), 1)
    group = lax.broadcasted_iota(jnp.int32, (asked, LANES), 1) // SLICE
    for block in range(BLOCKS):
        slab = slab_ref[block * PACK // N_FAR : (block + 1) * PACK // N_FAR].reshape(LANES, ROWS_DEV).T
        stack = jnp.concatenate(two_parts(slab), axis=1)
        total = jnp.zeros((asked, LANES), F32)
        for owner in range(PACK):
            z = block * PACK + owner
            onehot = jnp.where(ids[:, z : z + 1] == row, 1.0, 0.0).astype(BF16)
            both = dot(onehot, stack)
            total = jnp.where(group == owner, both[:, :LANES] + both[:, LANES:], total)
        for i in range(GROUP):
            out_ref[me_ref[0] ^ i, 0, block] = total[i * CAP : (i + 1) * CAP]


def serve_rows(me, ids, slab):
    return pl.pallas_call(
        serve_kernel,
        grid=(TABLES,),
        out_shape=jax.ShapeDtypeStruct((GROUP, TABLES, BLOCKS, CAP, LANES), F32),
        in_specs=[
            pl.BlockSpec(memory_space=pltpu.SMEM),
            pl.BlockSpec((GROUP, 1, CAP, N_HELD), lambda t: (0, t, 0, 0)),
            pl.BlockSpec((N_MID, N_FAR, SLICE, ROWS_DEV), lambda t: (0, 0, t, 0)),
        ],
        out_specs=pl.BlockSpec((GROUP, 1, BLOCKS, CAP, LANES), lambda t: (0, t, 0, 0, 0)),
        compiler_params=params(),
        name="serve_rows",
    )(me, ids, slab)


def count_kernel(inverse_ref, bag_ref, live_ref, count_ref, turned_ref):
    sample = lax.broadcasted_iota(jnp.int32, (SAMPLES, SLOTS), 0)
    unique = lax.broadcasted_iota(jnp.int32, (UNIQUE, SLOTS), 0)
    in_bag = jnp.where(sample == bag_ref[0], 1.0, 0.0).astype(BF16)
    in_slot = jnp.where(unique == inverse_ref[0], 1.0, 0.0).astype(BF16)
    counts = dot(in_bag, in_slot, ((1,), (1,)))
    count_ref[0] = (counts * live_ref[0]).astype(BF16)
    turned_ref[0] = counts.T.astype(BF16)


def count_slots(inverse, bag_ids, live):
    row = lambda t: (t, 0, 0)
    return pl.pallas_call(
        count_kernel,
        grid=(TABLES,),
        out_shape=[
            jax.ShapeDtypeStruct((TABLES, SAMPLES, UNIQUE), BF16),
            jax.ShapeDtypeStruct((TABLES, UNIQUE, SAMPLES), BF16),
        ],
        in_specs=[
            pl.BlockSpec((1, 1, SLOTS), row),
            pl.BlockSpec((1, 1, SLOTS), row),
            pl.BlockSpec((1, 1, UNIQUE), row),
        ],
        out_specs=[
            pl.BlockSpec((1, SAMPLES, UNIQUE), row),
            pl.BlockSpec((1, UNIQUE, SAMPLES), row),
        ],
        compiler_params=params(),
        name="count_slots",
    )(inverse, bag_ids, live)


def exchange_groups(tiles):
    group = lax.broadcasted_iota(jnp.int32, tiles[0].shape, 1) // SLICE
    step = PACK // 2
    while step:
        low_half = (group & step) == 0
        swapped = list(tiles)
        for i in range(PACK):
            if i & step == 0:
                a, b = tiles[i], tiles[i + step]
                swapped[i] = jnp.where(low_half, a, pltpu.roll(b, step * SLICE, 1))
                swapped[i + step] = jnp.where(low_half, pltpu.roll(a, LANES - step * SLICE, 1), b)
        tiles = swapped
        step //= 2
    return tiles


def tower_kernel(fetched_ref, count_ref, turned_ref, w_hidden_ref, bias_ref, w_out_ref, label_ref,
                 back_ref, feature_ref, grad_pre_ref, extra_ref, unique, pre):
    for t in range(TABLES):
        for source in range(N_NEAR * N_CORE):
            for half in range(N_DP // PACK):
                first = source * N_DP + half * PACK
                tiles = [fetched_ref[first + i, t].reshape(BLOCKS * CAP, LANES) for i in range(PACK)]
                for owner, tile in enumerate(exchange_groups(tiles)):
                    held = tile.reshape(BLOCKS, CAP, LANES)
                    for block in range(BLOCKS):
                        mid, far = divmod(block * PACK + owner, N_FAR)
                        unique[far, mid, source, :, half * LANES : (half + 1) * LANES] = held[block]
        high, low = two_parts(unique[...].reshape(UNIQUE, WIDTH))
        counts = count_ref[t]
        pooled = dot(counts, high) + dot(counts, low)
        feature_ref[:, t * WIDTH : (t + 1) * WIDTH] = pooled.astype(BF16)
    pre[...] = dot(feature_ref[...], w_hidden_ref[...]) + bias_ref[...]

    def chunk(i, sums):
        rows = pl.ds(pl.multiple_of(i * CHUNK, CHUNK), CHUNK)
        w_out = w_out_ref[...]
        x = pre[rows, :]
        sigma = jax.nn.sigmoid(x)
        hidden = x * sigma
        logit = jnp.sum(hidden * w_out, axis=1, keepdims=True)
        error = jax.nn.sigmoid(logit) - label_ref[rows, :].astype(F32)
        grad_pre = error * w_out * sigma * (1.0 + x * (1.0 - sigma))
        grad_pre_ref[rows, :] = grad_pre.astype(BF16)
        fold = lambda v: jnp.sum(v.reshape(CHUNK // 8, 8, HIDDEN), axis=0)
        return sums[0] + fold(grad_pre), sums[1] + fold(error * hidden)

    start = jnp.zeros((8, HIDDEN), F32)
    sums = lax.fori_loop(0, SAMPLES // CHUNK, chunk, (start, start))
    for which in range(2):
        row = jnp.sum(sums[which], axis=0, keepdims=True)
        for block in range(LANE_BLOCKS):
            at = which * LANE_BLOCKS + block
            extra_ref[at : at + 1, :] = row[:, block * LANES : (block + 1) * LANES]
    grad_pre = grad_pre_ref[...]
    for t in range(TABLES):
        grad = dot(grad_pre, w_hidden_ref[t * WIDTH : (t + 1) * WIDTH, :], ((1,), (1,)))
        high, low = two_parts(grad)
        turned = turned_ref[t]
        back_ref[:, t] = (dot(turned, high) + dot(turned, low)).reshape(N_TABLE, CAP, WIDTH)


def tower(fetched, counts, turned, w_hidden, b_hidden, w_out, labels):
    whole = pl.BlockSpec(memory_space=pltpu.VMEM)
    return pl.pallas_call(
        tower_kernel,
        out_shape=[
            jax.ShapeDtypeStruct((N_TABLE, TABLES, CAP, WIDTH), F32),
            jax.ShapeDtypeStruct((SAMPLES, FEATURES), BF16),
            jax.ShapeDtypeStruct((SAMPLES, HIDDEN), BF16),
            jax.ShapeDtypeStruct((8, LANES), F32),
        ],
        in_specs=[whole] * 7,
        out_specs=[whole] * 4,
        scratch_shapes=[
            pltpu.VMEM((N_FAR, N_MID, N_NEAR * N_CORE, CAP, WIDTH), F32),
            pltpu.VMEM((SAMPLES, HIDDEN), F32),
        ],
        compiler_params=params(),
        name="tower",
    )(fetched, counts, turned, w_hidden, b_hidden, w_out, labels)


def piece_rows(piece):
    return pl.ds(pl.multiple_of(piece * PIECE, 8), PIECE)


def lanes(block):
    return pl.ds(block * LANES, LANES)


def weight_kernel(me_ref, feature_ref, grad_pre_ref, extra_ref, out_ref, grad):
    grad[...] = dot(feature_ref[...], grad_pre_ref[...], ((0,), (0,)))
    for i in range(LAYER):
        for block in range(LANE_BLOCKS):
            out_ref[i, block * PIECE : (block + 1) * PIECE, :] = grad[piece_rows(me_ref[0] ^ i), lanes(block)]
        out_ref[i, PIECE_ROWS:, :] = extra_ref[...]


def weight_pieces(me, features, grad_pre, extra):
    whole = pl.BlockSpec(memory_space=pltpu.VMEM)
    return pl.pallas_call(
        weight_kernel,
        out_shape=jax.ShapeDtypeStruct((LAYER, SUM_ROWS, LANES), F32),
        in_specs=[pl.BlockSpec(memory_space=pltpu.SMEM)] + [whole] * 3,
        out_specs=whole,
        scratch_shapes=[pltpu.VMEM((FEATURES, HIDDEN), F32)],
        compiler_params=params(),
        name="weight_pieces",
    )(me, features, grad_pre, extra)


def unpack_kernel(me_ref, low_ref, high_ref, w_hidden_ref, bias_ref, w_out_ref):
    for i in range(LAYER):
        piece_ref = high_ref if i >= LAYER // 2 else low_ref
        for block in range(LANE_BLOCKS):
            w_hidden_ref[piece_rows(me_ref[0] ^ i), lanes(block)] = (
                piece_ref[i % (LAYER // 2), block * PIECE : (block + 1) * PIECE, :] / TOKENS
            )
    for block in range(LANE_BLOCKS):
        at = PIECE_ROWS + block
        bias_ref[:, lanes(block)] = low_ref[0, at : at + 1, :] / TOKENS
        at = at + LANE_BLOCKS
        w_out_ref[:, lanes(block)] = low_ref[0, at : at + 1, :] / TOKENS


def unpack(me, low, high):
    whole = pl.BlockSpec(memory_space=pltpu.VMEM)
    return pl.pallas_call(
        unpack_kernel,
        out_shape=[
            jax.ShapeDtypeStruct((FEATURES, HIDDEN), F32),
            jax.ShapeDtypeStruct((1, HIDDEN), F32),
            jax.ShapeDtypeStruct((1, HIDDEN), F32),
        ],
        in_specs=[pl.BlockSpec(memory_space=pltpu.SMEM)] + [whole] * 2,
        out_specs=[whole] * 3,
        compiler_params=params(),
        name="unpack",
    )(me, low, high)


def scatter_kernel(ids_ref, returned_ref, out_ref):
    row = lax.broadcasted_iota(jnp.int32, (ROWS_DEV, UNIQUE), 0)
    onehot = jnp.where(row == ids_ref[0], 1.0, 0.0).astype(BF16)
    high, low = two_parts(returned_ref[:, 0].reshape(UNIQUE, WIDTH))
    out_ref[0] = dot(onehot, high) + dot(onehot, low)


def scatter_rows(ids, returned):
    return pl.pallas_call(
        scatter_kernel,
        grid=(TABLES,),
        out_shape=jax.ShapeDtypeStruct((TABLES, ROWS_DEV, WIDTH), F32),
        in_specs=[
            pl.BlockSpec((1, 1, UNIQUE), lambda t: (t, 0, 0)),
            pl.BlockSpec((N_TABLE, 1, CAP, WIDTH), lambda t: (0, t, 0, 0)),
        ],
        out_specs=pl.BlockSpec((1, ROWS_DEV, WIDTH), lambda t: (t, 0, 0)),
        compiler_params=params(),
        name="scatter_rows",
    )(ids, returned)


def place(axes):
    return lax.axis_index(axes)


def swap(x, axes):
    return lax.all_to_all(x, axes, split_axis=0, concat_axis=0, tiled=True)


def spread(x, axes, count):
    return swap(jnp.broadcast_to(x[None], (count, *x.shape)), axes)


def partner(x, axis):
    return lax.ppermute(x, axis, [(0, 1), (1, 0)])


def pair_swap(x, axes):
    half = x.shape[0] // 2
    for axis in axes:
        x = jnp.stack([x[:half], partner(x[half:], axis)], axis=1).reshape(x.shape)
    return x


def pair_gather(x, axes):
    x = x[None]
    for axis in reversed(axes):
        x = jnp.concatenate([x, partner(x, axis)])
    return x


def relative(x, axes):
    shape = x.shape
    for at, axis in enumerate(axes):
        x = x.reshape(2**at, 2, -1, *shape[1:])
        x = jnp.where(lax.axis_index(axis) == 1, x[:, ::-1], x)
    return x.reshape(shape)


def pair_scatter_sum(x, axes):
    for axis in axes:
        half = x.shape[0] // 2
        x = x[:half] + partner(x[half:], axis)
    return x[0]


def quad_sum(x, axes):
    terms = [x] + [lax.ppermute(x, axes, [(i, i ^ k) for i in range(4)]) for k in range(1, 4)]
    return (terms[0] + terms[1]) + (terms[2] + terms[3])


def shards(emb_table, row_request, live_count, inverse, bag_ids, labels, w_hidden, b_hidden, w_out):
    request = row_request[0, 0]

    near = N_NEAR * N_CORE
    grouped = jnp.transpose(request.reshape(TABLES, N_FAR, N_MID, near, CAP), (3, 0, 4, 2, 1))
    grouped = relative(grouped.reshape(near, TABLES, CAP * N_HELD), ("near", "core"))
    grouped = pair_swap(grouped, ("near",))
    chip = grouped
    grouped = pair_swap(grouped, ("core",))
    ids = jnp.swapaxes(pair_gather(grouped, DP), 0, 1).reshape(GROUP, TABLES, CAP, N_HELD)

    every = jnp.transpose(request, (1, 0, 2)).reshape(N_TABLE, TABLES * CAP).astype(F32)
    every = jnp.pad(every, ((0, 0), (0, LANES // near - TABLES * CAP))).reshape(REQUEST_ROWS, WIDTH)
    slab = spread(slice_rows(place(DP).reshape(1), emb_table, every, chip), FAR, N_FAR)
    slab, ids = lax.optimization_barrier((slab, ids))
    slab = spread(slab, MID, N_MID)

    asked = slab[:, :, TABLES * SLICE :].reshape(N_HELD, REQUEST_ROWS, WIDTH)
    spot = place((*FAR, *MID))
    asked = lax.dynamic_slice(asked, (0, spot // 2, spot % 2 * LANES), (N_HELD, 1, LANES))
    asked = jnp.swapaxes(asked.reshape(N_HELD, near, LANES // near), 0, 1).astype(jnp.int32)
    asked = relative(pair_swap(relative(asked, ("near", "core")), ("near", "core")), ("near", "core"))
    asked = asked[:, :, : TABLES * CAP].reshape(near, N_MID, N_FAR, TABLES, CAP)
    asked = jnp.transpose(asked, (3, 2, 1, 0, 4)).reshape(TABLES, 1, UNIQUE)

    slot = lax.broadcasted_iota(jnp.int32, (TABLES, N_TABLE, CAP), 2)
    live = (slot < live_count[0, 0][:, :, None]).astype(F32).reshape(TABLES, 1, UNIQUE)
    counts, turned = count_slots(
        inverse[0, 0].reshape(TABLES, 1, SLOTS), bag_ids[0, 0].reshape(TABLES, 1, SLOTS), live
    )

    fetched = swap(serve_rows(place(SERVERS).reshape(1), ids, slab), SERVERS)
    fetched, asked = lax.optimization_barrier((fetched, asked))
    back, features, grad_pre, extra = tower(
        fetched,
        counts,
        turned,
        w_hidden,
        b_hidden.reshape(1, HIDDEN),
        w_out.reshape(1, HIDDEN),
        labels.reshape(SAMPLES, 1),
    )
    returned = swap(back, COLUMN)
    grad_shard = scatter_rows(asked, returned)

    me = place(SUMMERS).reshape(1)
    piece = pair_scatter_sum(weight_pieces(me, features, grad_pre, extra), SUMMERS)
    piece = piece + partner(piece, "near")
    piece = quad_sum(quad_sum(piece, MID), FAR)
    low = pair_gather(piece, SUMMERS[1:])
    grad_w, grad_b, grad_out = unpack(me, low, partner(low, SUMMERS[0]))
    return grad_shard[None], grad_w, grad_b.reshape(HIDDEN), grad_out.reshape(HIDDEN)


def solution(mesh):
    split = Mesh(mesh.devices.reshape((2,) * 10), (*COLUMN, *DP))
    return jax.shard_map(
        shards,
        mesh=split,
        in_specs=(
            P(None, COLUMN, None),
            P(COLUMN, DP, None, None, None),
            P(COLUMN, DP, None, None),
            P(COLUMN, DP, None, None),
            P(COLUMN, DP, None, None),
            P((*COLUMN, *DP)),
            P(),
            P(),
            P(),
        ),
        out_specs=(P(DP, None, COLUMN, None), P(), P(), P()),
        check_vma=False,
    )
```

time: 1380 us -> 447 us (0.32)
  waiting for transfers between devices: 831 us -> 216 us
  blocking collectives: 321 us -> 0 us
  other arithmetic: 173 us -> 1.8 us
  starting transfers between devices: 12.5 us -> 178 us
  Pallas kernels: 0 us -> 34.6 us
    psum x1 -> x0, waiting for transfers between devices: 680 us -> none  [shards(): lax.psum((term_w, term_b, term_out), ('table', 'dp'))]
    psum x1 -> x0, blocking collectives: 260 us -> none  [shards(): lax.psum((term_w, term_b, term_out), ('table', 'dp'))]
    ppermute x0 -> x25, waiting for transfers between devices: none -> 172 us  [the longest x19 145 us: partner(): return lax.ppermute(x, axis, [(0, 1), (1, 0)])]
    unnamed x10 -> x1, other arithmetic: 168 us -> 0.02 us
    ppermute x0 -> x25, starting transfers between devices: none -> 114 us  [the longest x19 73.9 us: partner(): return lax.ppermute(x, axis, [(0, 1), (1, 0)])]
    all_to_all x2 -> x4, waiting for transfers between devices: 151 us -> 43.9 us  [swap(): return lax.all_to_all(x, axes, split_axis=0, concat_axis=0, tiled=True)]
    all_to_all x1 -> x0, blocking collectives: 60.9 us -> none  [shards(): lax.all_to_all(request, 'table', split_axis=1, concat_axis=1, tiled=True)]
    all_to_all x2 -> x4, starting transfers between devices: 12.4 us -> 63.5 us  [swap(): return lax.all_to_all(x, axes, split_axis=0, concat_axis=0, tiled=True)]
  transfers between devices with their start and end apart: 3 -> 29, of which waited for: 2 -> 21; matrix products, arithmetic and copies ran while one was open for 1% -> 2% of each run, Pallas kernels for 0% -> 3%
where the time goes in v1:
time: 447 us; the launch traced here: 446 us
  waiting for transfers between devices  216 us (48%)
  starting transfers between devices  178 us (40%)
  Pallas kernels  34.6 us (8%)
  local copies, waits for them, and re-layouts  14.3 us (3%)
    ppermute x19, waiting for transfers between devices, partner(): return lax.ppermute(x, axis, [(0, 1), (1, 0)])  145 us
    ppermute x19, starting transfers between devices, partner(): return lax.ppermute(x, axis, [(0, 1), (1, 0)])  73.9 us
    all_to_all x4, starting transfers between devices, swap(): return lax.all_to_all(x, axes, split_axis=0, concat_axis=0, tiled=True)  63.5 us
    all_to_all x4, waiting for transfers between devices, swap(): return lax.all_to_all(x, axes, split_axis=0, concat_axis=0, tiled=True)  43.9 us
    ppermute x6, starting transfers between devices, quad_sum(): lax.ppermute(x, axes, [(i, i ^ k) for i in range(4)])  40.3 us
    ppermute x6, waiting for transfers between devices, quad_sum(): lax.ppermute(x, axes, [(i, i ^ k) for i in range(4)])  26.6 us
    pallas_call x1, Pallas kernels, tower(): pl.pallas_call(tower_kernel, out_shape=[jax.ShapeDtypeStruct((N_TABLE, TA...  11.1 us
  transfers between devices with their start and end apart: 29, of which 21 were waited for; matrix products, arithmetic and copies ran while one was open for 2% of the time, Pallas kernels for 3%

profile of v1, /device:TPU:1, one launch (start us, length us, event | category | flops | bytes accessed | tf_op | source)
XLA Modules:
  0.0 445.8 jit_solution(13949629216853704087)
XLA Ops:
  12.0 27.4 %all-to-all-start = ((f32[4,56,256]{2,1,0:T(8,128)}), f32[4,56,256]{2,1,0:T(8,128)S(1)}, u32[]{:S(2)}, u32[]{:S(2)}) async-start(f32[4,56,256]{2,1,0:T(8,128)} %broadcast_in_dim.8), calls=%async_computation | async-start | bytes 458752 | tf_op jit(solution)/shard_map/all_to_all | solution.py:321
  48.6 4.8 %collective-permute-start.3 = (s32[2,4,3,128]{3,1,2,0:T(4,128)S(1)}, s32[2,4,3,128]{3,1,2,0:T(4,128)S(1)}, u32[]{:S(2)}, u32[]{:S(2)}) collective-permute-start(s32[2,4,3,128]{3,1,2,0:T(4,128)S(1)} %pad_add_fusion.4), channel_id=1, source_target_pairs={{0,2},{2,0},{1,3},{3,1},{4,6},{6,4},{5,7},{7,5},{8,10},{10,8},{9,1... | collective-permute-start | bytes 36872 | tf_op jit(solution)/shard_map/ppermute | solution.py:329
  59.1 4.6 %collective-permute-start.5 = (s32[8,4,3,128]{3,1,2,0:T(4,128)S(1)}, s32[8,4,3,128]{3,1,2,0:T(4,128)S(1)}, u32[]{:S(2)}, u32[]{:S(2)}) collective-permute-start(s32[8,4,3,128]{3,1,2,0:T(4,128)S(1)} %pad_add_fusion), channel_id=1, source_target_pairs={{0,8},{8,0},{1,9},{9,1},{2,10},{10,2},{3,11},{11,3},{4,12},{12,4},... | collective-permute-start | bytes 147464 | tf_op jit(solution)/shard_map/ppermute | solution.py:329
  67.0 13.3 %all-to-all-start.1 = ((f32[4,4,56,256]{3,2,1,0:T(8,128)}), f32[4,4,56,256]{3,2,1,0:T(8,128)S(1)}, u32[]{:S(2)}, u32[]{:S(2)}) async-start(f32[4,4,56,256]{3,2,1,0:T(8,128)} %broadcast_in_dim.9), calls=%async_computation.1 | async-start | bytes 1835008 | tf_op jit(solution)/shard_map/all_to_all | solution.py:321
  81.3 43.9 %all-to-all-done.1.slab_ref = f32[4,4,56,256]{3,2,1,0:T(8,128)S(1)} async-done(((f32[4,4,56,256]{3,2,1,0:T(8,128)}), f32[4,4,56,256]{3,2,1,0:T(8,128)S(1)}, u32[]{:S(2)}, u32[]{:S(2)}) %all-to-all-start.1) | async-done | bytes 917536 | tf_op jit(solution)/shard_map/all_to_all | solution.py:321
  126.2 6.3 %serve_rows.1 = f32[64,3,2,8,128]{4,3,2,1,0:T(8,128)} custom-call(s32[1]{0:T(128)} %bitcast.me_ref, s32[64,3,8,16]{3,2,1,0:T(8,128)} %copy.57.ids_ref, f32[4,4,56,256]{3,2,1,0:T(8,128)} %copy-done.3), custom_call_target="tpu_custom_call" | custom-call | tf_op jit(solution)/shard_map/serve_rows/pallas_call | solution.py:104
  132.5 8.1 %all-to-all-start.2 = ((f32[64,3,2,8,128]{4,3,2,1,0:T(8,128)}), f32[64,3,2,8,128]{4,3,2,1,0:T(8,128)S(1)}, u32[]{:S(2)}, u32[]{:S(2)}) async-start(f32[64,3,2,8,128]{4,3,2,1,0:T(8,128)} %serve_rows.1), calls=%async_computation.2 | async-start | bytes 3145728 | tf_op jit(solution)/shard_map/all_to_all | solution.py:321
  144.7 15.4 %collective-permute-done.6 = s32[2,16,32]{2,1,0:T(8,128)S(1)} collective-permute-done((s32[2,16,32]{2,1,0:T(8,128)S(1)}, s32[2,16,32]{2,1,0:T(8,128)S(1)}, u32[]{:S(2)}, u32[]{:S(2)}) %collective-permute-start.6) | collective-permute-done | bytes 4128 | tf_op jit(solution)/shard_map/ppermute | solution.py:329
  164.3 5.8 %count_slots.1 = (bf16[3,512,512]{2,1,0:T(8,128)(2,1)}, bf16[3,512,512]{2,1,0:T(8,128)(2,1)}) custom-call(s32[3,1,2048]{2,1,0:T(1,128)} %bitcast.90, s32[3,1,2048]{2,1,0:T(1,128)} %bitcast.91, f32[3,1,512]{2,1,0:T(1,128)} %compare_convert_fusion.live_ref), custom_call_target="tpu_custom_call" | custom-call | tf_op jit(solution)/shard_map/count_slots/pallas_call | solution.py:131
  172.2 11.1 %tower.1 = (f32[64,3,8,256]{3,2,1,0:T(8,128)}, bf16[512,768]{1,0:T(8,128)(2,1)}, bf16[512,512]{1,0:T(8,128)(2,1)}, f32[8,128]{1,0:T(8,128)}) custom-call(f32[64,3,2,8,128]{4,3,2,1,0:T(8,128)} %copy-done.2, bf16[3,512,512]{2,1,0:T(8,128)(2,1)} %get-tuple-element.21.count_ref, bf16[3,512,512]{2,1,0:T(8,128)(2,1)} %get-tuple-element.22.turned_ref, ...), custom_call_target="tpu_custom_call" | custom-call | tf_op jit(solution)/shard_map/tower/pallas_call | solution.py:216
  183.3 14.7 %all-to-all-start.3 = ((f32[64,3,8,256]{3,2,1,0:T(8,128)}), f32[64,3,8,256]{3,2,1,0:T(8,128)S(1)}, u32[]{:S(2)}, u32[]{:S(2)}) async-start(f32[64,3,8,256]{3,2,1,0:T(8,128)} %get-tuple-element.23), calls=%async_computation.3 | async-start | bytes 3145728 | tf_op jit(solution)/shard_map/all_to_all | solution.py:321
  210.2 9.8 %collective-permute-done.9 = f32[8,104,128]{2,1,0:T(8,128)S(1)} collective-permute-done((f32[8,104,128]{2,1,0:T(8,128)S(1)}, f32[8,104,128]{2,1,0:T(8,128)S(1)}, u32[]{:S(2)}, u32[]{:S(2)}) %collective-permute-start.9) | collective-permute-done | bytes 426016 | tf_op jit(solution)/shard_map/ppermute | solution.py:329
  227.6 4.6 %collective-permute-start.11 = (f32[2,104,128]{2,1,0:T(8,128)S(1)}, f32[2,104,128]{2,1,0:T(8,128)S(1)}, u32[]{:S(2)}, u32[]{:S(2)}) collective-permute-start(f32[2,104,128]{2,1,0:T(8,128)S(1)} %slice.119), channel_id=1, source_target_pairs={{0,2},{2,0},{1,3},{3,1},{4,6},{6,4},{5,7},{7,5},{8,10},{10,8},{9,1... | collective-permute-start | bytes 319496 | tf_op jit(solution)/shard_map/ppermute | solution.py:329
  234.9 4.7 %collective-permute-start.12 = (f32[1,104,128]{2,1,0:T(8,128)S(1)}, f32[1,104,128]{2,1,0:T(8,128)S(1)}, u32[]{:S(2)}, u32[]{:S(2)}) collective-permute-start(f32[1,104,128]{2,1,0:T(8,128)S(1)} %slice.121), channel_id=1, source_target_pairs={{0,8},{8,0},{1,9},{9,1},{2,10},{10,2},{3,11},{11,3},{4,12},{12,4},... | collective-permute-start | bytes 159752 | tf_op jit(solution)/shard_map/ppermute | solution.py:329
  244.8 87.6 %collective-permute-done.13 = f32[104,128]{1,0:T(8,128)S(1)} collective-permute-done((f32[104,128]{1,0:T(8,128)S(1)}, f32[104,128]{1,0:T(8,128)S(1)}, u32[]{:S(2)}, u32[]{:S(2)}) %collective-permute-start.13) | collective-permute-done | bytes 53280 | tf_op jit(solution)/shard_map/ppermute | solution.py:329
  332.4 10.4 %collective-permute-start.16 = (f32[104,128]{1,0:T(8,128)S(1)}, f32[104,128]{1,0:T(8,128)S(1)}, u32[]{:S(2)}, u32[]{:S(2)}) collective-permute-start(f32[104,128]{1,0:T(8,128)S(1)} %add.108), channel_id=1, source_target_pairs={{0,192},{64,128},{128,64},{192,0},{1,193},{65,129},{129,65},{193,1... | collective-permute-start | bytes 159752 | tf_op jit(solution)/shard_map/ppermute | solution.py:362
  346.9 7.3 %collective-permute-done.15 = f32[104,128]{1,0:T(8,128)S(1)} collective-permute-done((f32[104,128]{1,0:T(8,128)S(1)}, f32[104,128]{1,0:T(8,128)S(1)}, u32[]{:S(2)}, u32[]{:S(2)}) %collective-permute-start.15) | collective-permute-done | bytes 53280 | tf_op jit(solution)/shard_map/ppermute | solution.py:362
  354.3 8.6 %collective-permute-start.19 = (f32[104,128]{1,0:T(8,128)S(1)}, f32[104,128]{1,0:T(8,128)S(1)}, u32[]{:S(2)}, u32[]{:S(2)}) collective-permute-start(f32[104,128]{1,0:T(8,128)S(1)} %add_add_fusion), channel_id=1, source_target_pairs={{0,768},{256,512},{512,256},{768,0},{1,769},{257,513},{513,257},{7... | collective-permute-start | bytes 159752 | tf_op jit(solution)/shard_map/ppermute | solution.py:362
  362.9 13.5 %collective-permute-start.18 = (f32[104,128]{1,0:T(8,128)S(1)}, f32[104,128]{1,0:T(8,128)S(1)}, u32[]{:S(2)}, u32[]{:S(2)}) collective-permute-start(f32[104,128]{1,0:T(8,128)S(1)} %add_add_fusion), channel_id=1, source_target_pairs={{0,512},{256,768},{512,0},{768,256},{1,513},{257,769},{513,1},{769... | collective-permute-start | bytes 159752 | tf_op jit(solution)/shard_map/ppermute | solution.py:362
  380.1 8.5 %collective-permute-done.18 = f32[104,128]{1,0:T(8,128)S(1)} collective-permute-done((f32[104,128]{1,0:T(8,128)S(1)}, f32[104,128]{1,0:T(8,128)S(1)}, u32[]{:S(2)}, u32[]{:S(2)}) %collective-permute-start.18) | collective-permute-done | bytes 53280 | tf_op jit(solution)/shard_map/ppermute | solution.py:362
  388.6 10.8 %collective-permute-done.17 = f32[104,128]{1,0:T(8,128)S(1)} collective-permute-done((f32[104,128]{1,0:T(8,128)S(1)}, f32[104,128]{1,0:T(8,128)S(1)}, u32[]{:S(2)}, u32[]{:S(2)}) %collective-permute-start.17) | collective-permute-done | bytes 53280 | tf_op jit(solution)/shard_map/ppermute | solution.py:362
  399.4 4.6 %collective-permute-start.20 = (f32[1,104,128]{2,1,0:T(8,128)S(1)}, f32[1,104,128]{2,1,0:T(8,128)S(1)}, u32[]{:S(2)}, u32[]{:S(2)}) collective-permute-start(f32[1,104,128]{2,1,0:T(8,128)S(1)} %get-tuple-element.31), channel_id=1, source_target_pairs={{0,8},{8,0},{1,9},{9,1},{2,10},{10,2},{3,11},{11,3},{4,12},{12,4},... | collective-permute-start | bytes 159752 | tf_op jit(solution)/shard_map/ppermute | solution.py:329
  422.6 6.1 %collective-permute-done.23 = f32[8,104,128]{2,1,0:T(8,128)S(1)} collective-permute-done((f32[8,104,128]{2,1,0:T(8,128)S(1)}, f32[8,104,128]{2,1,0:T(8,128)S(1)}, u32[]{:S(2)}, u32[]{:S(2)}) %collective-permute-start.23) | collective-permute-done | bytes 426016 | tf_op jit(solution)/shard_map/ppermute | solution.py:329
  428.7 6.8 %collective-permute-start.24 = (f32[16,104,128]{2,1,0:T(8,128)S(1)}, f32[16,104,128]{2,1,0:T(8,128)S(1)}, u32[]{:S(2)}, u32[]{:S(2)}) collective-permute-start(f32[16,104,128]{2,1,0:T(8,128)S(1)} %constant_dynamic-update-slice_fusion.5.low_ref), channel_id=1, source_target_pairs={{0,16},{16,0},{1,17},{17,1},{2,18},{18,2},{3,19},{19,3},{4,20},{20... | collective-permute-start | bytes 2555912 | tf_op jit(solution)/shard_map/ppermute | solution.py:329
  (130 shorter events, 105.6 us)
Async XLA Ops:
  12.0 54.0 %all-to-all-start = ((f32[4,56,256]{2,1,0:T(8,128)}), f32[4,56,256]{2,1,0:T(8,128)S(1)}, u32[]{:S(2)}, u32[]{:S(2)}) async-start(f32[4,56,256]{2,1,0:T(8,128)} %broadcast_in_dim.8), calls=%async_computation | async-start | bytes 458752 | tf_op jit(solution)/shard_map/all_to_all | solution.py:321
  48.6 5.9 %collective-permute-start.3 = (s32[2,4,3,128]{3,1,2,0:T(4,128)S(1)}, s32[2,4,3,128]{3,1,2,0:T(4,128)S(1)}, u32[]{:S(2)}, u32[]{:S(2)}) collective-permute-start(s32[2,4,3,128]{3,1,2,0:T(4,128)S(1)} %pad_add_fusion.4), channel_id=1, source_target_pairs={{0,2},{2,0},{1,3},{3,1},{4,6},{6,4},{5,7},{7,5},{8,10},{10,8},{9,1... | collective-permute-start | bytes 36872 | tf_op jit(solution)/shard_map/ppermute | solution.py:329
  59.1 6.6 %collective-permute-start.5 = (s32[8,4,3,128]{3,1,2,0:T(4,128)S(1)}, s32[8,4,3,128]{3,1,2,0:T(4,128)S(1)}, u32[]{:S(2)}, u32[]{:S(2)}) collective-permute-start(s32[8,4,3,128]{3,1,2,0:T(4,128)S(1)} %pad_add_fusion), channel_id=1, source_target_pairs={{0,8},{8,0},{1,9},{9,1},{2,10},{10,2},{3,11},{11,3},{4,12},{12,4},... | collective-permute-start | bytes 147464 | tf_op jit(solution)/shard_map/ppermute | solution.py:329
  67.0 58.2 %all-to-all-start.1 = ((f32[4,4,56,256]{3,2,1,0:T(8,128)}), f32[4,4,56,256]{3,2,1,0:T(8,128)S(1)}, u32[]{:S(2)}, u32[]{:S(2)}) async-start(f32[4,4,56,256]{3,2,1,0:T(8,128)} %broadcast_in_dim.9), calls=%async_computation.1 | async-start | bytes 1835008 | tf_op jit(solution)/shard_map/all_to_all | solution.py:321
  132.5 38.6 %all-to-all-start.2 = ((f32[64,3,2,8,128]{4,3,2,1,0:T(8,128)}), f32[64,3,2,8,128]{4,3,2,1,0:T(8,128)S(1)}, u32[]{:S(2)}, u32[]{:S(2)}) async-start(f32[64,3,2,8,128]{4,3,2,1,0:T(8,128)} %serve_rows.1), calls=%async_computation.2 | async-start | bytes 3145728 | tf_op jit(solution)/shard_map/all_to_all | solution.py:321
  140.9 19.2 %collective-permute-start.6 = (s32[2,16,32]{2,1,0:T(8,128)S(1)}, s32[2,16,32]{2,1,0:T(8,128)S(1)}, u32[]{:S(2)}, u32[]{:S(2)}) collective-permute-start(s32[2,16,32]{2,1,0:T(8,128)S(1)} %get-tuple-element.35), channel_id=1, source_target_pairs={{0,32},{32,0},{1,33},{33,1},{2,34},{34,2},{3,35},{35,3},{4,36},{36... | collective-permute-start | bytes 12296 | tf_op jit(solution)/shard_map/ppermute | solution.py:329
  160.1 10.0 %collective-permute-start.7 = (s32[2,16,32]{2,1,0:T(8,128)S(1)}, s32[2,16,32]{2,1,0:T(8,128)S(1)}, u32[]{:S(2)}, u32[]{:S(2)}) collective-permute-start(s32[2,16,32]{2,1,0:T(8,128)S(1)} %get-tuple-element.33), channel_id=1, source_target_pairs={{0,16},{16,0},{1,17},{17,1},{2,18},{18,2},{3,19},{19,3},{4,20},{20... | collective-permute-start | bytes 12296 | tf_op jit(solution)/shard_map/ppermute | solution.py:329
  183.3 257.7 %all-to-all-start.3 = ((f32[64,3,8,256]{3,2,1,0:T(8,128)}), f32[64,3,8,256]{3,2,1,0:T(8,128)S(1)}, u32[]{:S(2)}, u32[]{:S(2)}) async-start(f32[64,3,8,256]{3,2,1,0:T(8,128)} %get-tuple-element.23), calls=%async_computation.3 | async-start | bytes 3145728 | tf_op jit(solution)/shard_map/all_to_all | solution.py:321
  207.1 12.9 %collective-permute-start.9 = (f32[8,104,128]{2,1,0:T(8,128)S(1)}, f32[8,104,128]{2,1,0:T(8,128)S(1)}, u32[]{:S(2)}, u32[]{:S(2)}) collective-permute-start(f32[8,104,128]{2,1,0:T(8,128)S(1)} %slice.115), channel_id=1, source_target_pairs={{0,1},{1,0},{2,3},{3,2},{4,5},{5,4},{6,7},{7,6},{8,9},{9,8},{10,11... | collective-permute-start | bytes 1277960 | tf_op jit(solution)/shard_map/ppermute | solution.py:329
  220.1 7.4 %collective-permute-start.10 = (f32[4,104,128]{2,1,0:T(8,128)S(1)}, f32[4,104,128]{2,1,0:T(8,128)S(1)}, u32[]{:S(2)}, u32[]{:S(2)}) collective-permute-start(f32[4,104,128]{2,1,0:T(8,128)S(1)} %slice.117), channel_id=1, source_target_pairs={{0,4},{4,0},{1,5},{5,1},{2,6},{6,2},{3,7},{7,3},{8,12},{12,8},{9,1... | collective-permute-start | bytes 638984 | tf_op jit(solution)/shard_map/ppermute | solution.py:329
  227.6 7.2 %collective-permute-start.11 = (f32[2,104,128]{2,1,0:T(8,128)S(1)}, f32[2,104,128]{2,1,0:T(8,128)S(1)}, u32[]{:S(2)}, u32[]{:S(2)}) collective-permute-start(f32[2,104,128]{2,1,0:T(8,128)S(1)} %slice.119), channel_id=1, source_target_pairs={{0,2},{2,0},{1,3},{3,1},{4,6},{6,4},{5,7},{7,5},{8,10},{10,8},{9,1... | collective-permute-start | bytes 319496 | tf_op jit(solution)/shard_map/ppermute | solution.py:329
  234.9 6.4 %collective-permute-start.12 = (f32[1,104,128]{2,1,0:T(8,128)S(1)}, f32[1,104,128]{2,1,0:T(8,128)S(1)}, u32[]{:S(2)}, u32[]{:S(2)}) collective-permute-start(f32[1,104,128]{2,1,0:T(8,128)S(1)} %slice.121), channel_id=1, source_target_pairs={{0,8},{8,0},{1,9},{9,1},{2,10},{10,2},{3,11},{11,3},{4,12},{12,4},... | collective-permute-start | bytes 159752 | tf_op jit(solution)/shard_map/ppermute | solution.py:329
  241.2 91.1 %collective-permute-start.13 = (f32[104,128]{1,0:T(8,128)S(1)}, f32[104,128]{1,0:T(8,128)S(1)}, u32[]{:S(2)}, u32[]{:S(2)}) collective-permute-start(f32[104,128]{1,0:T(8,128)S(1)} %fusion), channel_id=1, source_target_pairs={{0,32},{32,0},{1,33},{33,1},{2,34},{34,2},{3,35},{35,3},{4,36},{36... | collective-permute-start | bytes 159752 | tf_op jit(solution)/shard_map/ppermute | solution.py:329
  332.4 14.6 %collective-permute-start.16 = (f32[104,128]{1,0:T(8,128)S(1)}, f32[104,128]{1,0:T(8,128)S(1)}, u32[]{:S(2)}, u32[]{:S(2)}) collective-permute-start(f32[104,128]{1,0:T(8,128)S(1)} %add.108), channel_id=1, source_target_pairs={{0,192},{64,128},{128,64},{192,0},{1,193},{65,129},{129,65},{193,1... | collective-permute-start | bytes 159752 | tf_op jit(solution)/shard_map/ppermute | solution.py:362
  342.8 11.5 %collective-permute-start.15 = (f32[104,128]{1,0:T(8,128)S(1)}, f32[104,128]{1,0:T(8,128)S(1)}, u32[]{:S(2)}, u32[]{:S(2)}) collective-permute-start(f32[104,128]{1,0:T(8,128)S(1)} %add.108), channel_id=1, source_target_pairs={{0,128},{64,192},{128,0},{192,64},{1,129},{65,193},{129,1},{193,65... | collective-permute-start | bytes 159752 | tf_op jit(solution)/shard_map/ppermute | solution.py:362
  344.7 9.6 %collective-permute-start.14 = (f32[104,128]{1,0:T(8,128)S(1)}, f32[104,128]{1,0:T(8,128)S(1)}, u32[]{:S(2)}, u32[]{:S(2)}) collective-permute-start(f32[104,128]{1,0:T(8,128)S(1)} %add.108), channel_id=1, source_target_pairs={{0,64},{64,0},{128,192},{192,128},{1,65},{65,1},{129,193},{193,129... | collective-permute-start | bytes 159752 | tf_op jit(solution)/shard_map/ppermute | solution.py:362
  354.3 25.8 %collective-permute-start.19 = (f32[104,128]{1,0:T(8,128)S(1)}, f32[104,128]{1,0:T(8,128)S(1)}, u32[]{:S(2)}, u32[]{:S(2)}) collective-permute-start(f32[104,128]{1,0:T(8,128)S(1)} %add_add_fusion), channel_id=1, source_target_pairs={{0,768},{256,512},{512,256},{768,0},{1,769},{257,513},{513,257},{7... | collective-permute-start | bytes 159752 | tf_op jit(solution)/shard_map/ppermute | solution.py:362
  362.9 25.7 %collective-permute-start.18 = (f32[104,128]{1,0:T(8,128)S(1)}, f32[104,128]{1,0:T(8,128)S(1)}, u32[]{:S(2)}, u32[]{:S(2)}) collective-permute-start(f32[104,128]{1,0:T(8,128)S(1)} %add_add_fusion), channel_id=1, source_target_pairs={{0,512},{256,768},{512,0},{768,256},{1,513},{257,769},{513,1},{769... | collective-permute-start | bytes 159752 | tf_op jit(solution)/shard_map/ppermute | solution.py:362
  376.4 23.0 %collective-permute-start.17 = (f32[104,128]{1,0:T(8,128)S(1)}, f32[104,128]{1,0:T(8,128)S(1)}, u32[]{:S(2)}, u32[]{:S(2)}) collective-permute-start(f32[104,128]{1,0:T(8,128)S(1)} %add_add_fusion), channel_id=1, source_target_pairs={{0,256},{256,0},{512,768},{768,512},{1,257},{257,1},{513,769},{769... | collective-permute-start | bytes 159752 | tf_op jit(solution)/shard_map/ppermute | solution.py:362
  399.4 6.4 %collective-permute-start.20 = (f32[1,104,128]{2,1,0:T(8,128)S(1)}, f32[1,104,128]{2,1,0:T(8,128)S(1)}, u32[]{:S(2)}, u32[]{:S(2)}) collective-permute-start(f32[1,104,128]{2,1,0:T(8,128)S(1)} %get-tuple-element.31), channel_id=1, source_target_pairs={{0,8},{8,0},{1,9},{9,1},{2,10},{10,2},{3,11},{11,3},{4,12},{12,4},... | collective-permute-start | bytes 159752 | tf_op jit(solution)/shard_map/ppermute | solution.py:329
  405.8 7.0 %collective-permute-start.21 = (f32[2,104,128]{2,1,0:T(8,128)S(1)}, f32[2,104,128]{2,1,0:T(8,128)S(1)}, u32[]{:S(2)}, u32[]{:S(2)}) collective-permute-start(f32[2,104,128]{2,1,0:T(8,128)S(1)} %pad_maximum_fusion.2), channel_id=1, source_target_pairs={{0,2},{2,0},{1,3},{3,1},{4,6},{6,4},{5,7},{7,5},{8,10},{10,8},{9,1... | collective-permute-start | bytes 319496 | tf_op jit(solution)/shard_map/ppermute | solution.py:329
  412.8 6.6 %collective-permute-start.22 = (f32[4,104,128]{2,1,0:T(8,128)S(1)}, f32[4,104,128]{2,1,0:T(8,128)S(1)}, u32[]{:S(2)}, u32[]{:S(2)}) collective-permute-start(f32[4,104,128]{2,1,0:T(8,128)S(1)} %pad_maximum_fusion.1), channel_id=1, source_target_pairs={{0,4},{4,0},{1,5},{5,1},{2,6},{6,2},{3,7},{7,3},{8,12},{12,8},{9,1... | collective-permute-start | bytes 638984 | tf_op jit(solution)/shard_map/ppermute | solution.py:329
  419.4 9.3 %collective-permute-start.23 = (f32[8,104,128]{2,1,0:T(8,128)S(1)}, f32[8,104,128]{2,1,0:T(8,128)S(1)}, u32[]{:S(2)}, u32[]{:S(2)}) collective-permute-start(f32[8,104,128]{2,1,0:T(8,128)S(1)} %pad_maximum_fusion), channel_id=1, source_target_pairs={{0,1},{1,0},{2,3},{3,2},{4,5},{5,4},{6,7},{7,6},{8,9},{9,8},{10,11... | collective-permute-start | bytes 1277960 | tf_op jit(solution)/shard_map/ppermute | solution.py:329
  428.7 8.8 %collective-permute-start.24 = (f32[16,104,128]{2,1,0:T(8,128)S(1)}, f32[16,104,128]{2,1,0:T(8,128)S(1)}, u32[]{:S(2)}, u32[]{:S(2)}) collective-permute-start(f32[16,104,128]{2,1,0:T(8,128)S(1)} %constant_dynamic-update-slice_fusion.5.low_ref), channel_id=1, source_target_pairs={{0,16},{16,0},{1,17},{17,1},{2,18},{18,2},{3,19},{19,3},{4,20},{20... | collective-permute-start | bytes 2555912 | tf_op jit(solution)/shard_map/ppermute | solution.py:329
  (14 other events, 93.6 us)

commit v2 on v1

--- a/solution.py
+++ b/solution.py
@@ -33,15 +33,16 @@
 FEATURES = TABLES * WIDTH
 TOKENS = SAMPLES * N_TABLE * N_DP
 LANE_BLOCKS = HIDDEN // LANES
-PIECE = FEATURES // LAYER
-PIECE_ROWS = PIECE * LANE_BLOCKS
+PIECE = FEATURES // (GROUP // 2)
+HALF_BLOCKS = LANE_BLOCKS // 2
+PIECE_ROWS = PIECE * HALF_BLOCKS
 SUM_ROWS = PIECE_ROWS + 8
 FAR = ("far1", "far0")
 MID = ("mid1", "mid0")
 COLUMN = (*FAR, *MID, "near", "core")
 DP = ("x1", "x0", "y1", "y0")
 SERVERS = ("near", "core", *DP)
-SUMMERS = ("core", "y0", "x0", "y1", "x1")
+SUMMERS = ("core", "y0", "x0", "y1", "x1", "near")
 CHUNK = 32
 VMEM = 56 * 1024 * 1024
 
@@ -59,36 +60,39 @@
     return lax.dot_general(a, b, (dims, ((), ())), preferred_element_type=F32)
 
 
-def slice_kernel(dp_ref, table_ref, request_ref, after_ref, out_ref, turned):
+def slice_kernel(dp_ref, table_ref, request_ref, out_ref, turned):
     dp = dp_ref[0]
     half = pl.multiple_of(dp // PACK * LANES, LANES)
     first = pl.multiple_of(dp % PACK * SLICE, SLICE)
     for t in range(TABLES):
         turned[...] = table_ref[t, :, pl.ds(half, LANES)].T
         out_ref[t * SLICE : (t + 1) * SLICE] = turned[pl.ds(first, SLICE), :]
-    out_ref[TABLES * SLICE :] = request_ref[...]
-
-
-def slice_rows(dp, emb_table, requests, after):
+    out_ref[TABLES * SLICE :, :LANES] = request_ref[:REQUEST_ROWS]
+    out_ref[TABLES * SLICE :, LANES:] = request_ref[REQUEST_ROWS:]
+
+
+def slice_rows(dp, emb_table, requests):
     whole = pl.BlockSpec(memory_space=pltpu.VMEM)
     return pl.pallas_call(
         slice_kernel,
         out_shape=jax.ShapeDtypeStruct((TABLES * SLICE + REQUEST_ROWS, ROWS_DEV), F32),
-        in_specs=[pl.BlockSpec(memory_space=pltpu.SMEM), whole, whole, pl.BlockSpec(memory_space=pl.ANY)],
+        in_specs=[pl.BlockSpec(memory_space=pltpu.SMEM), whole, whole],
         out_specs=whole,
         scratch_shapes=[pltpu.VMEM((LANES, ROWS_DEV), F32)],
         compiler_params=params(),
         name="slice_rows",
-    )(dp, emb_table, requests, after)
-
-
-def serve_kernel(me_ref, ids_ref, slab_ref, out_ref):
+    )(dp, emb_table, requests)
+
+
+def serve_kernel(me_ref, mid_ref, ids_ref, slab_ref, out_ref):
     asked = GROUP * CAP
     ids = ids_ref[:, 0].reshape(asked, N_HELD)
     row = lax.broadcasted_iota(jnp.int32, (asked, ROWS_DEV), 1)
     group = lax.broadcasted_iota(jnp.int32, (asked, LANES), 1) // SLICE
     for block in range(BLOCKS):
-        slab = slab_ref[block * PACK // N_FAR : (block + 1) * PACK // N_FAR].reshape(LANES, ROWS_DEV).T
+        mids = range(block * PACK // N_FAR, (block + 1) * PACK // N_FAR)
+        slab = [slab_ref[(mid + N_MID - mid_ref[0]) % N_MID].reshape(N_FAR * SLICE, ROWS_DEV) for mid in mids]
+        slab = jnp.concatenate(slab).T
         stack = jnp.concatenate(two_parts(slab), axis=1)
         total = jnp.zeros((asked, LANES), F32)
         for owner in range(PACK):
@@ -100,20 +104,21 @@
             out_ref[me_ref[0] ^ i, 0, block] = total[i * CAP : (i + 1) * CAP]
 
 
-def serve_rows(me, ids, slab):
+def serve_rows(me, mid, ids, slab):
     return pl.pallas_call(
         serve_kernel,
         grid=(TABLES,),
         out_shape=jax.ShapeDtypeStruct((GROUP, TABLES, BLOCKS, CAP, LANES), F32),
         in_specs=[
             pl.BlockSpec(memory_space=pltpu.SMEM),
+            pl.BlockSpec(memory_space=pltpu.SMEM),
             pl.BlockSpec((GROUP, 1, CAP, N_HELD), lambda t: (0, t, 0, 0)),
             pl.BlockSpec((N_MID, N_FAR, SLICE, ROWS_DEV), lambda t: (0, 0, t, 0)),
         ],
         out_specs=pl.BlockSpec((GROUP, 1, BLOCKS, CAP, LANES), lambda t: (0, t, 0, 0, 0)),
         compiler_params=params(),
         name="serve_rows",
-    )(me, ids, slab)
+    )(me, mid, ids, slab)
 
 
 def count_kernel(inverse_ref, bag_ref, live_ref, count_ref, turned_ref):
@@ -232,19 +237,18 @@
     )(fetched, counts, turned, w_hidden, b_hidden, w_out, labels)
 
 
-def piece_rows(piece):
-    return pl.ds(pl.multiple_of(piece * PIECE, 8), PIECE)
-
-
-def lanes(block):
-    return pl.ds(block * LANES, LANES)
+def piece_at(piece, block):
+    rows = pl.ds(pl.multiple_of((piece >> 1) * PIECE, 8), PIECE)
+    columns = pl.ds(pl.multiple_of(((piece & 1) * HALF_BLOCKS + block) * LANES, LANES), LANES)
+    return rows, columns
 
 
 def weight_kernel(me_ref, feature_ref, grad_pre_ref, extra_ref, out_ref, grad):
     grad[...] = dot(feature_ref[...], grad_pre_ref[...], ((0,), (0,)))
-    for i in range(LAYER):
-        for block in range(LANE_BLOCKS):
-            out_ref[i, block * PIECE : (block + 1) * PIECE, :] = grad[piece_rows(me_ref[0] ^ i), lanes(block)]
+    for i in range(GROUP):
+        for block in range(HALF_BLOCKS):
+            rows, columns = piece_at(me_ref[0] ^ i, block)
+            out_ref[i, block * PIECE : (block + 1) * PIECE, :] = grad[rows, columns]
         out_ref[i, PIECE_ROWS:, :] = extra_ref[...]
 
 
@@ -252,7 +256,7 @@
     whole = pl.BlockSpec(memory_space=pltpu.VMEM)
     return pl.pallas_call(
         weight_kernel,
-        out_shape=jax.ShapeDtypeStruct((LAYER, SUM_ROWS, LANES), F32),
+        out_shape=jax.ShapeDtypeStruct((GROUP, SUM_ROWS, LANES), F32),
         in_specs=[pl.BlockSpec(memory_space=pltpu.SMEM)] + [whole] * 3,
         out_specs=whole,
         scratch_shapes=[pltpu.VMEM((FEATURES, HIDDEN), F32)],
@@ -262,17 +266,19 @@
 
 
 def unpack_kernel(me_ref, low_ref, high_ref, w_hidden_ref, bias_ref, w_out_ref):
-    for i in range(LAYER):
-        piece_ref = high_ref if i >= LAYER // 2 else low_ref
-        for block in range(LANE_BLOCKS):
-            w_hidden_ref[piece_rows(me_ref[0] ^ i), lanes(block)] = (
-                piece_ref[i % (LAYER // 2), block * PIECE : (block + 1) * PIECE, :] / TOKENS
+    for i in range(GROUP):
+        piece_ref = high_ref if i >= GROUP // 2 else low_ref
+        for block in range(HALF_BLOCKS):
+            rows, columns = piece_at(me_ref[0] ^ i, block)
+            w_hidden_ref[rows, columns] = (
+                piece_ref[i % (GROUP // 2), block * PIECE : (block + 1) * PIECE, :] / TOKENS
             )
     for block in range(LANE_BLOCKS):
         at = PIECE_ROWS + block
-        bias_ref[:, lanes(block)] = low_ref[0, at : at + 1, :] / TOKENS
+        columns = pl.ds(block * LANES, LANES)
+        bias_ref[:, columns] = low_ref[0, at : at + 1, :] / TOKENS
         at = at + LANE_BLOCKS
-        w_out_ref[:, lanes(block)] = low_ref[0, at : at + 1, :] / TOKENS
+        w_out_ref[:, columns] = low_ref[0, at : at + 1, :] / TOKENS
 
 
 def unpack(me, low, high):
@@ -358,9 +364,15 @@
     return x[0]
 
 
-def quad_sum(x, axes):
-    terms = [x] + [lax.ppermute(x, axes, [(i, i ^ k) for i in range(4)]) for k in range(1, 4)]
-    return (terms[0] + terms[1]) + (terms[2] + terms[3])
+def shift(x, axes, count, by):
+    return lax.ppermute(x, axes, [(i, (i + by) % count) for i in range(count)])
+
+
+def sum_over_z(x):
+    for axis in reversed(MID):
+        x = x + partner(x, axis)
+    x = x + partner(x, FAR[1])
+    return x + lax.ppermute(x, FAR, [(i, N_FAR - 1 - i) for i in range(N_FAR)])
 
 
 def shards(emb_table, row_request, live_count, inverse, bag_ids, labels, w_hidden, b_hidden, w_out):
@@ -369,23 +381,24 @@
     near = N_NEAR * N_CORE
     grouped = jnp.transpose(request.reshape(TABLES, N_FAR, N_MID, near, CAP), (3, 0, 4, 2, 1))
     grouped = relative(grouped.reshape(near, TABLES, CAP * N_HELD), ("near", "core"))
-    grouped = pair_swap(grouped, ("near",))
-    chip = grouped
-    grouped = pair_swap(grouped, ("core",))
+    grouped = pair_swap(grouped, ("near", "core"))
     ids = jnp.swapaxes(pair_gather(grouped, DP), 0, 1).reshape(GROUP, TABLES, CAP, N_HELD)
 
-    every = jnp.transpose(request, (1, 0, 2)).reshape(N_TABLE, TABLES * CAP).astype(F32)
-    every = jnp.pad(every, ((0, 0), (0, LANES // near - TABLES * CAP))).reshape(REQUEST_ROWS, WIDTH)
-    slab = spread(slice_rows(place(DP).reshape(1), emb_table, every, chip), FAR, N_FAR)
+    travel = grouped.reshape(near * TABLES, CAP * N_HELD).astype(F32)
+    travel = jnp.pad(travel, ((0, 2 * REQUEST_ROWS - near * TABLES), (0, 0)))
+    slab = spread(slice_rows(place(DP).reshape(1), emb_table, travel), FAR, N_FAR)
     slab, ids = lax.optimization_barrier((slab, ids))
-    slab = spread(slab, MID, N_MID)
-
-    asked = slab[:, :, TABLES * SLICE :].reshape(N_HELD, REQUEST_ROWS, WIDTH)
-    spot = place((*FAR, *MID))
-    asked = lax.dynamic_slice(asked, (0, spot // 2, spot % 2 * LANES), (N_HELD, 1, LANES))
-    asked = jnp.swapaxes(asked.reshape(N_HELD, near, LANES // near), 0, 1).astype(jnp.int32)
-    asked = relative(pair_swap(relative(asked, ("near", "core")), ("near", "core")), ("near", "core"))
-    asked = asked[:, :, : TABLES * CAP].reshape(near, N_MID, N_FAR, TABLES, CAP)
+    held = (*FAR, *MID)
+    across = [shift(slab[: N_FAR // 2], held, N_HELD, -2), shift(slab[N_FAR // 2 :], held, N_HELD, 2)]
+    slab = jnp.stack([slab, shift(slab, held, N_HELD, -1), jnp.concatenate(across), shift(slab, held, N_HELD, 1)])
+
+    mid = place(MID)
+    asked = slab[:, :, TABLES * SLICE :]
+    asked = jnp.concatenate([asked[..., :LANES], asked[..., LANES:]], axis=2)[:, :, : near * TABLES]
+    asked = asked.reshape(N_MID, N_FAR, near, TABLES, CAP, N_HELD)
+    asked = lax.dynamic_index_in_dim(asked, mid * N_FAR + place(FAR), 5, keepdims=False).astype(jnp.int32)
+    asked = lax.dynamic_slice_in_dim(jnp.concatenate([asked, asked]), (N_MID - mid) % N_MID, N_MID, axis=0)
+    asked = relative(jnp.moveaxis(asked, 2, 0), ("near", "core"))
     asked = jnp.transpose(asked, (3, 2, 1, 0, 4)).reshape(TABLES, 1, UNIQUE)
 
     slot = lax.broadcasted_iota(jnp.int32, (TABLES, N_TABLE, CAP), 2)
@@ -394,7 +407,8 @@
         inverse[0, 0].reshape(TABLES, 1, SLOTS), bag_ids[0, 0].reshape(TABLES, 1, SLOTS), live
     )
 
-    fetched = swap(serve_rows(place(SERVERS).reshape(1), ids, slab), SERVERS)
+    slab, counts, turned = lax.optimization_barrier((slab, counts, turned))
+    fetched = swap(serve_rows(place(SERVERS).reshape(1), mid.reshape(1), ids, slab), SERVERS)
     fetched, asked = lax.optimization_barrier((fetched, asked))
     back, features, grad_pre, extra = tower(
         fetched,
@@ -410,9 +424,7 @@
 
     me = place(SUMMERS).reshape(1)
     piece = pair_scatter_sum(weight_pieces(me, features, grad_pre, extra), SUMMERS)
-    piece = piece + partner(piece, "near")
-    piece = quad_sum(quad_sum(piece, MID), FAR)
-    low = pair_gather(piece, SUMMERS[1:])
+    low = pair_gather(sum_over_z(piece), SUMMERS[1:])
     grad_w, grad_b, grad_out = unpack(me, low, partner(low, SUMMERS[0]))
     return grad_shard[None], grad_w, grad_b.reshape(HIDDEN), grad_out.reshape(HIDDEN)
 

time: 447 us -> 408 us (0.913)
  waiting for transfers between devices: 216 us -> 170 us
  starting transfers between devices: 178 us -> 184 us
    ppermute x19 -> x21, starting transfers between devices: 73.9 us -> 101 us  [partner(): return lax.ppermute(x, axis, [(0, 1), (1, 0)])]
    ppermute x6 -> x5, waiting for transfers between devices: 26.6 us -> 1.36 us  [the longest x1 1.35 us: sum_over_z(): return x + lax.ppermute(x, FAR, [(i, N_FAR - 1 - i) for i in range(N_FAR)])]
    all_to_all x4 -> x3, waiting for transfers between devices: 43.9 us -> 19.1 us  [swap(): return lax.all_to_all(x, axes, split_axis=0, concat_axis=0, tiled=True)]
    all_to_all x4 -> x3, starting transfers between devices: 63.5 us -> 43.4 us  [swap(): return lax.all_to_all(x, axes, split_axis=0, concat_axis=0, tiled=True)]
    ppermute x19 -> x21, waiting for transfers between devices: 145 us -> 149 us  [partner(): return lax.ppermute(x, axis, [(0, 1), (1, 0)])]
    ppermute x6 -> x5, starting transfers between devices: 40.3 us -> 40.2 us  [the longest x4 25.2 us: shift(): return lax.ppermute(x, axes, [(i, (i + by) % count) for i in range(count)])]
  transfers between devices with their start and end apart: 29 -> 29, of which waited for: 21 -> 24; matrix products, arithmetic and copies ran while one was open for 2% -> 2% of each run, Pallas kernels for 3% -> 3%
where the time goes in v2:
time: 408 us; the launch traced here: 407 us
  starting transfers between devices  184 us (45%)
  waiting for transfers between devices  170 us (42%)
  Pallas kernels  34.9 us (9%)
  local copies, waits for them, and re-layouts  14.1 us (3%)
    ppermute x21, waiting for transfers between devices, partner(): return lax.ppermute(x, axis, [(0, 1), (1, 0)])  149 us
    ppermute x21, starting transfers between devices, partner(): return lax.ppermute(x, axis, [(0, 1), (1, 0)])  101 us
    all_to_all x3, starting transfers between devices, swap(): return lax.all_to_all(x, axes, split_axis=0, concat_axis=0, tiled=True)  43.4 us
    ppermute x4, starting transfers between devices, shift(): return lax.ppermute(x, axes, [(i, (i + by) % count) for i in range(count)])  25.2 us
    all_to_all x3, waiting for transfers between devices, swap(): return lax.all_to_all(x, axes, split_axis=0, concat_axis=0, tiled=True)  19.1 us
    ppermute x1, starting transfers between devices, sum_over_z(): return x + lax.ppermute(x, FAR, [(i, N_FAR - 1 - i) for i in range(N_FAR)])  14.9 us
    pallas_call x1, Pallas kernels, tower(): pl.pallas_call(tower_kernel, out_shape=[jax.ShapeDtypeStruct((N_TABLE, TA...  11.1 us
  transfers between devices with their start and end apart: 29, of which 24 were waited for; matrix products, arithmetic and copies ran while one was open for 2% of the time, Pallas kernels for 3%

profile of v2, /device:TPU:1, one launch (start us, length us, event | category | flops | bytes accessed | tf_op | source)
XLA Modules:
  0.0 406.5 jit_solution(13536869360914565545)
XLA Ops:
  2.1 4.4 %collective-permute-start = (s32[2,3,128]{2,0,1:T(2,128)S(1)}, s32[2,3,128]{2,0,1:T(2,128)S(1)}, u32[]{:S(2)}, u32[]{:S(2)}) collective-permute-start(s32[2,3,128]{2,0,1:T(2,128)S(1)} %get-tuple-element.55), channel_id=1, source_target_pairs={{0,32},{32,0},{1,33},{33,1},{2,34},{34,2},{3,35},{35,3},{4,36},{36... | collective-permute-start | bytes 9224 | tf_op jit(solution)/shard_map/ppermute | solution.py:335
  7.5 16.2 %collective-permute-start.1 = (s32[2,3,128]{2,0,1:T(2,128)S(1)}, s32[2,3,128]{2,0,1:T(2,128)S(1)}, u32[]{:S(2)}, u32[]{:S(2)}) collective-permute-start(s32[2,3,128]{2,0,1:T(2,128)S(1)} %bitcast.82), channel_id=1, source_target_pairs={{0,16},{16,0},{1,17},{17,1},{2,18},{18,2},{3,19},{19,3},{4,20},{20... | collective-permute-start | bytes 9224 | tf_op jit(solution)/shard_map/ppermute | solution.py:335
  28.6 15.4 %all-to-all-start = ((f32[4,56,256]{2,1,0:T(8,128)}), f32[4,56,256]{2,1,0:T(8,128)S(1)}, u32[]{:S(2)}, u32[]{:S(2)}) async-start(f32[4,56,256]{2,1,0:T(8,128)} %broadcast_in_dim.12), calls=%async_computation | async-start | bytes 458752 | tf_op jit(solution)/shard_map/all_to_all | solution.py:327
  48.7 4.8 %collective-permute-start.3 = (s32[2,4,3,128]{3,1,2,0:T(4,128)S(1)}, s32[2,4,3,128]{3,1,2,0:T(4,128)S(1)}, u32[]{:S(2)}, u32[]{:S(2)}) collective-permute-start(s32[2,4,3,128]{3,1,2,0:T(4,128)S(1)} %pad_add_fusion.2), channel_id=1, source_target_pairs={{0,2},{2,0},{1,3},{3,1},{4,6},{6,4},{5,7},{7,5},{8,10},{10,8},{9,1... | collective-permute-start | bytes 36872 | tf_op jit(solution)/shard_map/ppermute | solution.py:335
  59.5 4.6 %collective-permute-start.5 = (s32[8,4,3,128]{3,1,2,0:T(4,128)S(1)}, s32[8,4,3,128]{3,1,2,0:T(4,128)S(1)}, u32[]{:S(2)}, u32[]{:S(2)}) collective-permute-start(s32[8,4,3,128]{3,1,2,0:T(4,128)S(1)} %pad_add_fusion), channel_id=1, source_target_pairs={{0,8},{8,0},{1,9},{9,1},{2,10},{10,2},{3,11},{11,3},{4,12},{12,4},... | collective-permute-start | bytes 147464 | tf_op jit(solution)/shard_map/ppermute | solution.py:335
  68.0 6.6 %collective-permute-start.9 = (f32[4,56,256]{2,1,0:T(8,128)S(1)}, f32[4,56,256]{2,1,0:T(8,128)S(1)}, u32[]{:S(2)}, u32[]{:S(2)}) collective-permute-start(f32[4,56,256]{2,1,0:T(8,128)S(1)} %all-to-all-done), channel_id=1, source_target_pairs={{0,64},{64,128},{128,192},{192,256},{256,320},{320,384},{384,448},... | collective-permute-start | bytes 688136 | tf_op jit(solution)/shard_map/ppermute | solution.py:368
  74.6 9.4 %collective-permute-start.6 = (f32[4,56,256]{2,1,0:T(8,128)S(1)}, f32[4,56,256]{2,1,0:T(8,128)S(1)}, u32[]{:S(2)}, u32[]{:S(2)}) collective-permute-start(f32[4,56,256]{2,1,0:T(8,128)S(1)} %all-to-all-done), channel_id=1, source_target_pairs={{0,960},{64,0},{128,64},{192,128},{256,192},{320,256},{384,320},{4... | collective-permute-start | bytes 688136 | tf_op jit(solution)/shard_map/ppermute | solution.py:368
  84.1 4.0 collective-permute-start.7
  88.1 5.2 %collective-permute-start.8 = (f32[2,56,256]{2,1,0:T(8,128)S(1)}, f32[2,56,256]{2,1,0:T(8,128)S(1)}, u32[]{:S(2)}, u32[]{:S(2)}) collective-permute-start(f32[2,56,256]{2,1,0:T(8,128)S(1)} %get-tuple-element.43), channel_id=1, source_target_pairs={{0,128},{64,192},{128,256},{192,320},{256,384},{320,448},{384,512}... | collective-permute-start | bytes 344072 | tf_op jit(solution)/shard_map/ppermute | solution.py:368
  93.9 5.8 %count_slots.1 = (bf16[3,512,512]{2,1,0:T(8,128)(2,1)}, bf16[3,512,512]{2,1,0:T(8,128)(2,1)}) custom-call(s32[3,1,2048]{2,1,0:T(1,128)} %bitcast.79, s32[3,1,2048]{2,1,0:T(1,128)} %bitcast.80, f32[3,1,512]{2,1,0:T(1,128)} %compare_convert_fusion.live_ref), custom_call_target="tpu_custom_call" | custom-call | tf_op jit(solution)/shard_map/count_slots/pallas_call | solution.py:136
  101.7 6.3 %serve_rows.1 = f32[64,3,2,8,128]{4,3,2,1,0:T(8,128)} custom-call(s32[1]{0:T(128)} %bitcast.me_ref, s32[1]{0:T(128)} %bitcast.1.mid_ref, s32[64,3,8,16]{3,2,1,0:T(8,128)} %copy.66.ids_ref, f32[4,4,56,256]{3,2,1,0:T(8,128)} %pad_maximum_fusion.slab_ref), custom_call_target="tpu_custom_call" | custom-call | tf_op jit(solution)/shard_map/serve_rows/pallas_call | solution.py:108
  108.1 16.6 %all-to-all-start.1 = ((f32[64,3,2,8,128]{4,3,2,1,0:T(8,128)}), f32[64,3,2,8,128]{4,3,2,1,0:T(8,128)S(1)}, u32[]{:S(2)}, u32[]{:S(2)}) async-start(f32[64,3,2,8,128]{4,3,2,1,0:T(8,128)} %serve_rows.1), calls=%async_computation.1 | async-start | bytes 3145728 | tf_op jit(solution)/shard_map/all_to_all | solution.py:327
  129.3 17.4 %all-to-all-done.1.fetched_ref = f32[64,3,2,8,128]{4,3,2,1,0:T(8,128)S(1)} async-done(((f32[64,3,2,8,128]{4,3,2,1,0:T(8,128)}), f32[64,3,2,8,128]{4,3,2,1,0:T(8,128)S(1)}, u32[]{:S(2)}, u32[]{:S(2)}) %all-to-all-start.1) | async-done | bytes 1572896 | tf_op jit(solution)/shard_map/all_to_all | solution.py:327
  147.9 11.1 %tower.1 = (f32[64,3,8,256]{3,2,1,0:T(8,128)}, bf16[512,768]{1,0:T(8,128)(2,1)}, bf16[512,512]{1,0:T(8,128)(2,1)}, f32[8,128]{1,0:T(8,128)}) custom-call(f32[64,3,2,8,128]{4,3,2,1,0:T(8,128)} %copy-done.2, bf16[3,512,512]{2,1,0:T(8,128)(2,1)} %get-tuple-element.27.count_ref, bf16[3,512,512]{2,1,0:T(8,128)(2,1)} %get-tuple-element.28.turned_ref, ...), custom_call_target="tpu_custom_call" | custom-call | tf_op jit(solution)/shard_map/tower/pallas_call | solution.py:221
  159.0 11.4 %all-to-all-start.2 = ((f32[64,3,8,256]{3,2,1,0:T(8,128)}), f32[64,3,8,256]{3,2,1,0:T(8,128)S(1)}, u32[]{:S(2)}, u32[]{:S(2)}) async-start(f32[64,3,8,256]{3,2,1,0:T(8,128)} %get-tuple-element.29), calls=%async_computation.2 | async-start | bytes 3145728 | tf_op jit(solution)/shard_map/all_to_all | solution.py:327
  182.4 11.2 %collective-permute-done.11 = f32[16,56,128]{2,1,0:T(8,128)S(1)} collective-permute-done((f32[16,56,128]{2,1,0:T(8,128)S(1)}, f32[16,56,128]{2,1,0:T(8,128)S(1)}, u32[]{:S(2)}, u32[]{:S(2)}) %collective-permute-start.11) | collective-permute-done | bytes 458784 | tf_op jit(solution)/shard_map/ppermute | solution.py:335
  195.9 5.6 %collective-permute-done.12 = f32[8,56,128]{2,1,0:T(8,128)S(1)} collective-permute-done((f32[8,56,128]{2,1,0:T(8,128)S(1)}, f32[8,56,128]{2,1,0:T(8,128)S(1)}, u32[]{:S(2)}, u32[]{:S(2)}) %collective-permute-start.12) | collective-permute-done | bytes 229408 | tf_op jit(solution)/shard_map/ppermute | solution.py:335
  218.7 85.4 %collective-permute-done.15 = f32[1,56,128]{2,1,0:T(8,128)S(1)} collective-permute-done((f32[1,56,128]{2,1,0:T(8,128)S(1)}, f32[1,56,128]{2,1,0:T(8,128)S(1)}, u32[]{:S(2)}, u32[]{:S(2)}) %collective-permute-start.15) | collective-permute-done | bytes 28704 | tf_op jit(solution)/shard_map/ppermute | solution.py:335
  310.3 8.0 %collective-permute-start.17 = (f32[56,128]{1,0:T(8,128)S(1)}, f32[56,128]{1,0:T(8,128)S(1)}, u32[]{:S(2)}, u32[]{:S(2)}) collective-permute-start(f32[56,128]{1,0:T(8,128)S(1)} %add.107), channel_id=1, source_target_pairs={{0,128},{128,0},{1,129},{129,1},{2,130},{130,2},{3,131},{131,3},{4... | collective-permute-start | bytes 86024 | tf_op jit(solution)/shard_map/ppermute | solution.py:335
  319.9 12.0 %collective-permute-start.18 = (f32[56,128]{1,0:T(8,128)S(1)}, f32[56,128]{1,0:T(8,128)S(1)}, u32[]{:S(2)}, u32[]{:S(2)}) collective-permute-start(f32[56,128]{1,0:T(8,128)S(1)} %add.108), channel_id=1, source_target_pairs={{0,256},{256,0},{1,257},{257,1},{2,258},{258,2},{3,259},{259,3},{4... | collective-permute-start | bytes 86024 | tf_op jit(solution)/shard_map/ppermute | solution.py:335
  333.2 14.9 %collective-permute-start.19 = (f32[56,128]{1,0:T(8,128)S(1)}, f32[56,128]{1,0:T(8,128)S(1)}, u32[]{:S(2)}, u32[]{:S(2)}) collective-permute-start(f32[56,128]{1,0:T(8,128)S(1)} %add.109), channel_id=1, source_target_pairs={{0,768},{256,512},{512,256},{768,0},{1,769},{257,513},{513,257},{7... | collective-permute-start | bytes 86024 | tf_op jit(solution)/shard_map/ppermute | solution.py:375
  370.2 4.8 %collective-permute-done.23 = f32[8,56,128]{2,1,0:T(8,128)S(1)} collective-permute-done((f32[8,56,128]{2,1,0:T(8,128)S(1)}, f32[8,56,128]{2,1,0:T(8,128)S(1)}, u32[]{:S(2)}, u32[]{:S(2)}) %collective-permute-start.23) | collective-permute-done | bytes 229408 | tf_op jit(solution)/shard_map/ppermute | solution.py:335
  377.5 6.8 %collective-permute-done.24 = f32[16,56,128]{2,1,0:T(8,128)S(1)} collective-permute-done((f32[16,56,128]{2,1,0:T(8,128)S(1)}, f32[16,56,128]{2,1,0:T(8,128)S(1)}, u32[]{:S(2)}, u32[]{:S(2)}) %collective-permute-start.24) | collective-permute-done | bytes 458784 | tf_op jit(solution)/shard_map/ppermute | solution.py:335
  384.3 11.6 %collective-permute-start.25 = (f32[32,56,128]{2,1,0:T(8,128)S(1)}, f32[32,56,128]{2,1,0:T(8,128)S(1)}, u32[]{:S(2)}, u32[]{:S(2)}) collective-permute-start(f32[32,56,128]{2,1,0:T(8,128)S(1)} %constant_dynamic-update-slice_fusion.10.low_ref), channel_id=1, source_target_pairs={{0,16},{16,0},{1,17},{17,1},{2,18},{18,2},{3,19},{19,3},{4,20},{20... | collective-permute-start | bytes 2752520 | tf_op jit(solution)/shard_map/ppermute | solution.py:335
  (128 shorter events, 105.5 us)
Async XLA Ops:
  7.5 17.0 %collective-permute-start.1 = (s32[2,3,128]{2,0,1:T(2,128)S(1)}, s32[2,3,128]{2,0,1:T(2,128)S(1)}, u32[]{:S(2)}, u32[]{:S(2)}) collective-permute-start(s32[2,3,128]{2,0,1:T(2,128)S(1)} %bitcast.82), channel_id=1, source_target_pairs={{0,16},{16,0},{1,17},{17,1},{2,18},{18,2},{3,19},{19,3},{4,20},{20... | collective-permute-start | bytes 9224 | tf_op jit(solution)/shard_map/ppermute | solution.py:335
  28.6 39.5 %all-to-all-start = ((f32[4,56,256]{2,1,0:T(8,128)}), f32[4,56,256]{2,1,0:T(8,128)S(1)}, u32[]{:S(2)}, u32[]{:S(2)}) async-start(f32[4,56,256]{2,1,0:T(8,128)} %broadcast_in_dim.12), calls=%async_computation | async-start | bytes 458752 | tf_op jit(solution)/shard_map/all_to_all | solution.py:327
  48.7 6.2 %collective-permute-start.3 = (s32[2,4,3,128]{3,1,2,0:T(4,128)S(1)}, s32[2,4,3,128]{3,1,2,0:T(4,128)S(1)}, u32[]{:S(2)}, u32[]{:S(2)}) collective-permute-start(s32[2,4,3,128]{3,1,2,0:T(4,128)S(1)} %pad_add_fusion.2), channel_id=1, source_target_pairs={{0,2},{2,0},{1,3},{3,1},{4,6},{6,4},{5,7},{7,5},{8,10},{10,8},{9,1... | collective-permute-start | bytes 36872 | tf_op jit(solution)/shard_map/ppermute | solution.py:335
  59.5 6.6 %collective-permute-start.5 = (s32[8,4,3,128]{3,1,2,0:T(4,128)S(1)}, s32[8,4,3,128]{3,1,2,0:T(4,128)S(1)}, u32[]{:S(2)}, u32[]{:S(2)}) collective-permute-start(s32[8,4,3,128]{3,1,2,0:T(4,128)S(1)} %pad_add_fusion), channel_id=1, source_target_pairs={{0,8},{8,0},{1,9},{9,1},{2,10},{10,2},{3,11},{11,3},{4,12},{12,4},... | collective-permute-start | bytes 147464 | tf_op jit(solution)/shard_map/ppermute | solution.py:335
  68.0 32.6 %collective-permute-start.9 = (f32[4,56,256]{2,1,0:T(8,128)S(1)}, f32[4,56,256]{2,1,0:T(8,128)S(1)}, u32[]{:S(2)}, u32[]{:S(2)}) collective-permute-start(f32[4,56,256]{2,1,0:T(8,128)S(1)} %all-to-all-done), channel_id=1, source_target_pairs={{0,64},{64,128},{128,192},{192,256},{256,320},{320,384},{384,448},... | collective-permute-start | bytes 688136 | tf_op jit(solution)/shard_map/ppermute | solution.py:368
  74.6 26.0 %collective-permute-start.6 = (f32[4,56,256]{2,1,0:T(8,128)S(1)}, f32[4,56,256]{2,1,0:T(8,128)S(1)}, u32[]{:S(2)}, u32[]{:S(2)}) collective-permute-start(f32[4,56,256]{2,1,0:T(8,128)S(1)} %all-to-all-done), channel_id=1, source_target_pairs={{0,960},{64,0},{128,64},{192,128},{256,192},{320,256},{384,320},{4... | collective-permute-start | bytes 688136 | tf_op jit(solution)/shard_map/ppermute | solution.py:368
  84.1 16.5 %collective-permute-start.7 = (f32[2,56,256]{2,1,0:T(8,128)S(1)}, f32[2,56,256]{2,1,0:T(8,128)S(1)}, u32[]{:S(2)}, u32[]{:S(2)}) collective-permute-start(f32[2,56,256]{2,1,0:T(8,128)S(1)} %get-tuple-element.42), channel_id=1, source_target_pairs={{0,896},{64,960},{128,0},{192,64},{256,128},{320,192},{384,256},{4... | collective-permute-start | bytes 344072 | tf_op jit(solution)/shard_map/ppermute | solution.py:368
  88.1 12.5 %collective-permute-start.8 = (f32[2,56,256]{2,1,0:T(8,128)S(1)}, f32[2,56,256]{2,1,0:T(8,128)S(1)}, u32[]{:S(2)}, u32[]{:S(2)}) collective-permute-start(f32[2,56,256]{2,1,0:T(8,128)S(1)} %get-tuple-element.43), channel_id=1, source_target_pairs={{0,128},{64,192},{128,256},{192,320},{256,384},{320,448},{384,512}... | collective-permute-start | bytes 344072 | tf_op jit(solution)/shard_map/ppermute | solution.py:368
  108.1 38.7 %all-to-all-start.1 = ((f32[64,3,2,8,128]{4,3,2,1,0:T(8,128)}), f32[64,3,2,8,128]{4,3,2,1,0:T(8,128)S(1)}, u32[]{:S(2)}, u32[]{:S(2)}) async-start(f32[64,3,2,8,128]{4,3,2,1,0:T(8,128)} %serve_rows.1), calls=%async_computation.1 | async-start | bytes 3145728 | tf_op jit(solution)/shard_map/all_to_all | solution.py:327
  159.0 242.8 %all-to-all-start.2 = ((f32[64,3,8,256]{3,2,1,0:T(8,128)}), f32[64,3,8,256]{3,2,1,0:T(8,128)S(1)}, u32[]{:S(2)}, u32[]{:S(2)}) async-start(f32[64,3,8,256]{3,2,1,0:T(8,128)} %get-tuple-element.29), calls=%async_computation.2 | async-start | bytes 3145728 | tf_op jit(solution)/shard_map/all_to_all | solution.py:327
  180.0 13.6 %collective-permute-start.11 = (f32[16,56,128]{2,1,0:T(8,128)S(1)}, f32[16,56,128]{2,1,0:T(8,128)S(1)}, u32[]{:S(2)}, u32[]{:S(2)}) collective-permute-start(f32[16,56,128]{2,1,0:T(8,128)S(1)} %slice.106), channel_id=1, source_target_pairs={{0,1},{1,0},{2,3},{3,2},{4,5},{5,4},{6,7},{7,6},{8,9},{9,8},{10,11... | collective-permute-start | bytes 1376264 | tf_op jit(solution)/shard_map/ppermute | solution.py:335
  193.7 7.8 %collective-permute-start.12 = (f32[8,56,128]{2,1,0:T(8,128)S(1)}, f32[8,56,128]{2,1,0:T(8,128)S(1)}, u32[]{:S(2)}, u32[]{:S(2)}) collective-permute-start(f32[8,56,128]{2,1,0:T(8,128)S(1)} %slice.108), channel_id=1, source_target_pairs={{0,4},{4,0},{1,5},{5,1},{2,6},{6,2},{3,7},{7,3},{8,12},{12,8},{9,1... | collective-permute-start | bytes 688136 | tf_op jit(solution)/shard_map/ppermute | solution.py:335
  201.5 7.3 %collective-permute-start.13 = (f32[4,56,128]{2,1,0:T(8,128)S(1)}, f32[4,56,128]{2,1,0:T(8,128)S(1)}, u32[]{:S(2)}, u32[]{:S(2)}) collective-permute-start(f32[4,56,128]{2,1,0:T(8,128)S(1)} %slice.110), channel_id=1, source_target_pairs={{0,2},{2,0},{1,3},{3,1},{4,6},{6,4},{5,7},{7,5},{8,10},{10,8},{9,1... | collective-permute-start | bytes 344072 | tf_op jit(solution)/shard_map/ppermute | solution.py:335
  208.9 6.7 %collective-permute-start.14 = (f32[2,56,128]{2,1,0:T(8,128)S(1)}, f32[2,56,128]{2,1,0:T(8,128)S(1)}, u32[]{:S(2)}, u32[]{:S(2)}) collective-permute-start(f32[2,56,128]{2,1,0:T(8,128)S(1)} %slice.112), channel_id=1, source_target_pairs={{0,8},{8,0},{1,9},{9,1},{2,10},{10,2},{3,11},{11,3},{4,12},{12,4},... | collective-permute-start | bytes 172040 | tf_op jit(solution)/shard_map/ppermute | solution.py:335
  215.6 88.5 %collective-permute-start.15 = (f32[1,56,128]{2,1,0:T(8,128)S(1)}, f32[1,56,128]{2,1,0:T(8,128)S(1)}, u32[]{:S(2)}, u32[]{:S(2)}) collective-permute-start(f32[1,56,128]{2,1,0:T(8,128)S(1)} %slice.114), channel_id=1, source_target_pairs={{0,32},{32,0},{1,33},{33,1},{2,34},{34,2},{3,35},{35,3},{4,36},{36... | collective-permute-start | bytes 86024 | tf_op jit(solution)/shard_map/ppermute | solution.py:335
  304.1 6.2 %collective-permute-start.16 = (f32[56,128]{1,0:T(8,128)S(1)}, f32[56,128]{1,0:T(8,128)S(1)}, u32[]{:S(2)}, u32[]{:S(2)}) collective-permute-start(f32[56,128]{1,0:T(8,128)S(1)} %fusion.2), channel_id=1, source_target_pairs={{0,64},{64,0},{1,65},{65,1},{2,66},{66,2},{3,67},{67,3},{4,68},{68... | collective-permute-start | bytes 86024 | tf_op jit(solution)/shard_map/ppermute | solution.py:335
  310.3 9.5 %collective-permute-start.17 = (f32[56,128]{1,0:T(8,128)S(1)}, f32[56,128]{1,0:T(8,128)S(1)}, u32[]{:S(2)}, u32[]{:S(2)}) collective-permute-start(f32[56,128]{1,0:T(8,128)S(1)} %add.107), channel_id=1, source_target_pairs={{0,128},{128,0},{1,129},{129,1},{2,130},{130,2},{3,131},{131,3},{4... | collective-permute-start | bytes 86024 | tf_op jit(solution)/shard_map/ppermute | solution.py:335
  319.9 13.3 %collective-permute-start.18 = (f32[56,128]{1,0:T(8,128)S(1)}, f32[56,128]{1,0:T(8,128)S(1)}, u32[]{:S(2)}, u32[]{:S(2)}) collective-permute-start(f32[56,128]{1,0:T(8,128)S(1)} %add.108), channel_id=1, source_target_pairs={{0,256},{256,0},{1,257},{257,1},{2,258},{258,2},{3,259},{259,3},{4... | collective-permute-start | bytes 86024 | tf_op jit(solution)/shard_map/ppermute | solution.py:335
  333.2 16.3 %collective-permute-start.19 = (f32[56,128]{1,0:T(8,128)S(1)}, f32[56,128]{1,0:T(8,128)S(1)}, u32[]{:S(2)}, u32[]{:S(2)}) collective-permute-start(f32[56,128]{1,0:T(8,128)S(1)} %add.109), channel_id=1, source_target_pairs={{0,768},{256,512},{512,256},{768,0},{1,769},{257,513},{513,257},{7... | collective-permute-start | bytes 86024 | tf_op jit(solution)/shard_map/ppermute | solution.py:375
  354.4 6.4 %collective-permute-start.21 = (f32[2,56,128]{2,1,0:T(8,128)S(1)}, f32[2,56,128]{2,1,0:T(8,128)S(1)}, u32[]{:S(2)}, u32[]{:S(2)}) collective-permute-start(f32[2,56,128]{2,1,0:T(8,128)S(1)} %pad_maximum_fusion.4), channel_id=1, source_target_pairs={{0,8},{8,0},{1,9},{9,1},{2,10},{10,2},{3,11},{11,3},{4,12},{12,4},... | collective-permute-start | bytes 172040 | tf_op jit(solution)/shard_map/ppermute | solution.py:335
  360.9 7.0 %collective-permute-start.22 = (f32[4,56,128]{2,1,0:T(8,128)S(1)}, f32[4,56,128]{2,1,0:T(8,128)S(1)}, u32[]{:S(2)}, u32[]{:S(2)}) collective-permute-start(f32[4,56,128]{2,1,0:T(8,128)S(1)} %pad_maximum_fusion.3), channel_id=1, source_target_pairs={{0,2},{2,0},{1,3},{3,1},{4,6},{6,4},{5,7},{7,5},{8,10},{10,8},{9,1... | collective-permute-start | bytes 344072 | tf_op jit(solution)/shard_map/ppermute | solution.py:335
  367.9 7.1 %collective-permute-start.23 = (f32[8,56,128]{2,1,0:T(8,128)S(1)}, f32[8,56,128]{2,1,0:T(8,128)S(1)}, u32[]{:S(2)}, u32[]{:S(2)}) collective-permute-start(f32[8,56,128]{2,1,0:T(8,128)S(1)} %pad_maximum_fusion.1), channel_id=1, source_target_pairs={{0,4},{4,0},{1,5},{5,1},{2,6},{6,2},{3,7},{7,3},{8,12},{12,8},{9,1... | collective-permute-start | bytes 688136 | tf_op jit(solution)/shard_map/ppermute | solution.py:335
  375.0 9.2 %collective-permute-start.24 = (f32[16,56,128]{2,1,0:T(8,128)S(1)}, f32[16,56,128]{2,1,0:T(8,128)S(1)}, u32[]{:S(2)}, u32[]{:S(2)}) collective-permute-start(f32[16,56,128]{2,1,0:T(8,128)S(1)} %get-tuple-element.40), channel_id=1, source_target_pairs={{0,1},{1,0},{2,3},{3,2},{4,5},{5,4},{6,7},{7,6},{8,9},{9,8},{10,11... | collective-permute-start | bytes 1376264 | tf_op jit(solution)/shard_map/ppermute | solution.py:335
  384.3 13.7 %collective-permute-start.25 = (f32[32,56,128]{2,1,0:T(8,128)S(1)}, f32[32,56,128]{2,1,0:T(8,128)S(1)}, u32[]{:S(2)}, u32[]{:S(2)}) collective-permute-start(f32[32,56,128]{2,1,0:T(8,128)S(1)} %constant_dynamic-update-slice_fusion.10.low_ref), channel_id=1, source_target_pairs={{0,16},{16,0},{1,17},{17,1},{2,18},{18,2},{3,19},{19,3},{4,20},{20... | collective-permute-start | bytes 2752520 | tf_op jit(solution)/shard_map/ppermute | solution.py:335
  (12 other events, 106.8 us)

commit v3 on v2

--- a/solution.py
+++ b/solution.py
@@ -45,10 +45,11 @@
 SUMMERS = ("core", "y0", "x0", "y1", "x1", "near")
 CHUNK = 32
 VMEM = 56 * 1024 * 1024
-
-
-def params():
-    return pltpu.CompilerParams(vmem_limit_bytes=VMEM)
+LESS_VMEM = 16 * 1024 * 1024
+
+
+def params(limit=VMEM):
+    return pltpu.CompilerParams(vmem_limit_bytes=limit)
 
 
 def two_parts(x):
@@ -66,22 +67,28 @@
     first = pl.multiple_of(dp % PACK * SLICE, SLICE)
     for t in range(TABLES):
         turned[...] = table_ref[t, :, pl.ds(half, LANES)].T
-        out_ref[t * SLICE : (t + 1) * SLICE] = turned[pl.ds(first, SLICE), :]
-    out_ref[TABLES * SLICE :, :LANES] = request_ref[:REQUEST_ROWS]
-    out_ref[TABLES * SLICE :, LANES:] = request_ref[REQUEST_ROWS:]
+        for far in range(N_FAR):
+            out_ref[far, t * SLICE : (t + 1) * SLICE] = turned[pl.ds(first, SLICE), :]
+    for far in range(N_FAR):
+        out_ref[far, TABLES * SLICE :, :LANES] = request_ref[:REQUEST_ROWS]
+        out_ref[far, TABLES * SLICE :, LANES:] = request_ref[REQUEST_ROWS:]
 
 
 def slice_rows(dp, emb_table, requests):
     whole = pl.BlockSpec(memory_space=pltpu.VMEM)
     return pl.pallas_call(
         slice_kernel,
-        out_shape=jax.ShapeDtypeStruct((TABLES * SLICE + REQUEST_ROWS, ROWS_DEV), F32),
+        out_shape=jax.ShapeDtypeStruct((N_FAR, TABLES * SLICE + REQUEST_ROWS, ROWS_DEV), F32),
         in_specs=[pl.BlockSpec(memory_space=pltpu.SMEM), whole, whole],
         out_specs=whole,
         scratch_shapes=[pltpu.VMEM((LANES, ROWS_DEV), F32)],
         compiler_params=params(),
         name="slice_rows",
     )(dp, emb_table, requests)
+
+
+def server_offset(i):
+    return i ^ ((i >> 1) & 0b000101)
 
 
 def serve_kernel(me_ref, mid_ref, ids_ref, slab_ref, out_ref):
@@ -101,7 +108,7 @@
             both = dot(onehot, stack)
             total = jnp.where(group == owner, both[:, :LANES] + both[:, LANES:], total)
         for i in range(GROUP):
-            out_ref[me_ref[0] ^ i, 0, block] = total[i * CAP : (i + 1) * CAP]
+            out_ref[me_ref[0] ^ server_offset(i), 0, block] = total[i * CAP : (i + 1) * CAP]
 
 
 def serve_rows(me, mid, ids, slab):
@@ -292,7 +299,7 @@
         ],
         in_specs=[pl.BlockSpec(memory_space=pltpu.SMEM)] + [whole] * 2,
         out_specs=[whole] * 3,
-        compiler_params=params(),
+        compiler_params=params(LESS_VMEM),
         name="unpack",
     )(me, low, high)
 
@@ -314,7 +321,7 @@
             pl.BlockSpec((N_TABLE, 1, CAP, WIDTH), lambda t: (0, t, 0, 0)),
         ],
         out_specs=pl.BlockSpec((1, ROWS_DEV, WIDTH), lambda t: (t, 0, 0)),
-        compiler_params=params(),
+        compiler_params=params(LESS_VMEM),
         name="scatter_rows",
     )(ids, returned)
 
@@ -327,12 +334,20 @@
     return lax.all_to_all(x, axes, split_axis=0, concat_axis=0, tiled=True)
 
 
-def spread(x, axes, count):
-    return swap(jnp.broadcast_to(x[None], (count, *x.shape)), axes)
-
-
 def partner(x, axis):
+    if axis in ("x1", "y1"):
+        return lax.ppermute(x, (axis, axis[0] + "0"), [(i, 3 - i) for i in range(4)])
     return lax.ppermute(x, axis, [(0, 1), (1, 0)])
+
+
+def pair_place(axes):
+    index = 0
+    for axis in axes:
+        bit = lax.axis_index(axis)
+        if axis in ("x0", "y0"):
+            bit = bit ^ lax.axis_index(axis[0] + "1")
+        index = index * 2 + bit
+    return index
 
 
 def pair_swap(x, axes):
@@ -343,7 +358,6 @@
 
 
 def pair_gather(x, axes):
-    x = x[None]
     for axis in reversed(axes):
         x = jnp.concatenate([x, partner(x, axis)])
     return x
@@ -382,11 +396,11 @@
     grouped = jnp.transpose(request.reshape(TABLES, N_FAR, N_MID, near, CAP), (3, 0, 4, 2, 1))
     grouped = relative(grouped.reshape(near, TABLES, CAP * N_HELD), ("near", "core"))
     grouped = pair_swap(grouped, ("near", "core"))
-    ids = jnp.swapaxes(pair_gather(grouped, DP), 0, 1).reshape(GROUP, TABLES, CAP, N_HELD)
+    ids = jnp.swapaxes(pair_gather(grouped[None], DP), 0, 1).reshape(GROUP, TABLES, CAP, N_HELD)
 
     travel = grouped.reshape(near * TABLES, CAP * N_HELD).astype(F32)
     travel = jnp.pad(travel, ((0, 2 * REQUEST_ROWS - near * TABLES), (0, 0)))
-    slab = spread(slice_rows(place(DP).reshape(1), emb_table, travel), FAR, N_FAR)
+    slab = swap(slice_rows(place(DP).reshape(1), emb_table, travel), FAR)
     slab, ids = lax.optimization_barrier((slab, ids))
     held = (*FAR, *MID)
     across = [shift(slab[: N_FAR // 2], held, N_HELD, -2), shift(slab[N_FAR // 2 :], held, N_HELD, 2)]
@@ -419,13 +433,12 @@
         w_out.reshape(1, HIDDEN),
         labels.reshape(SAMPLES, 1),
     )
-    returned = swap(back, COLUMN)
-    grad_shard = scatter_rows(asked, returned)
-
-    me = place(SUMMERS).reshape(1)
+    grad_shard = scatter_rows(asked, swap(back, COLUMN))
+    me = pair_place(SUMMERS).reshape(1)
     piece = pair_scatter_sum(weight_pieces(me, features, grad_pre, extra), SUMMERS)
-    low = pair_gather(sum_over_z(piece), SUMMERS[1:])
-    grad_w, grad_b, grad_out = unpack(me, low, partner(low, SUMMERS[0]))
+    low = pair_gather(sum_over_z(piece)[None], SUMMERS[1:])
+    high, grad_shard = lax.optimization_barrier((partner(low, SUMMERS[0]), grad_shard))
+    grad_w, grad_b, grad_out = unpack(me, low, high)
     return grad_shard[None], grad_w, grad_b.reshape(HIDDEN), grad_out.reshape(HIDDEN)
 
 

time: 408 us -> 398 us (0.975)
  local copies, waits for them, and re-layouts: 14.1 us -> 9.86 us
    ppermute x21 -> x15, starting transfers between devices: 101 us -> 78 us  [partner(): return lax.ppermute(x, axis, [(0, 1), (1, 0)])]
    ppermute x0 -> x6, starting transfers between devices: none -> 20.5 us  [partner(): lax.ppermute(x, (axis, axis[0] + '0'), [(i, 3 - i) for i in range(4)])]
    ppermute x21 -> x15, waiting for transfers between devices: 149 us -> 130 us  [partner(): return lax.ppermute(x, axis, [(0, 1), (1, 0)])]
    ppermute x0 -> x6, waiting for transfers between devices: none -> 18 us  [partner(): lax.ppermute(x, (axis, axis[0] + '0'), [(i, 3 - i) for i in range(4)])]
  transfers between devices with their start and end apart: 29 -> 29, of which waited for: 24 -> 23; matrix products, arithmetic and copies ran while one was open for 2% -> 2% of each run, Pallas kernels for 3% -> 3%
where the time goes in v3:
time: 398 us; the launch traced here: 396 us
  starting transfers between devices  181 us (45%)
  waiting for transfers between devices  170 us (43%)
  Pallas kernels  32.1 us (8%)
  local copies, waits for them, and re-layouts  9.86 us (2%)
    ppermute x15, waiting for transfers between devices, partner(): return lax.ppermute(x, axis, [(0, 1), (1, 0)])  130 us
    ppermute x15, starting transfers between devices, partner(): return lax.ppermute(x, axis, [(0, 1), (1, 0)])  78 us
    all_to_all x3, starting transfers between devices, swap(): return lax.all_to_all(x, axes, split_axis=0, concat_axis=0, tiled=True)  42.5 us
    ppermute x4, starting transfers between devices, shift(): return lax.ppermute(x, axes, [(i, (i + by) % count) for i in range(count)])  25.2 us
    ppermute x6, starting transfers between devices, partner(): lax.ppermute(x, (axis, axis[0] + '0'), [(i, 3 - i) for i in range(4)])  20.5 us
    all_to_all x3, waiting for transfers between devices, swap(): return lax.all_to_all(x, axes, split_axis=0, concat_axis=0, tiled=True)  20.1 us
    ppermute x6, waiting for transfers between devices, partner(): lax.ppermute(x, (axis, axis[0] + '0'), [(i, 3 - i) for i in range(4)])  18 us
    ppermute x1, starting transfers between devices, sum_over_z(): return x + lax.ppermute(x, FAR, [(i, N_FAR - 1 - i) for i in range(N_FAR)])  14.9 us
  transfers between devices with their start and end apart: 29, of which 23 were waited for; matrix products, arithmetic and copies ran while one was open for 2% of the time, Pallas kernels for 3%

profile of v3, /device:TPU:1, one launch (start us, length us, event | category | flops | bytes accessed | tf_op | source)
XLA Modules:
  0.0 396.5 jit_solution(10822168693821469358)
XLA Ops:
  2.1 4.4 %collective-permute-start = (s32[2,3,128]{2,0,1:T(2,128)S(1)}, s32[2,3,128]{2,0,1:T(2,128)S(1)}, u32[]{:S(2)}, u32[]{:S(2)}) collective-permute-start(s32[2,3,128]{2,0,1:T(2,128)S(1)} %get-tuple-element.59), channel_id=1, source_target_pairs={{0,32},{32,0},{1,33},{33,1},{2,34},{34,2},{3,35},{35,3},{4,36},{36... | collective-permute-start | bytes 9224 | tf_op jit(solution)/shard_map/ppermute | solution.py:340
  7.5 16.2 %collective-permute-start.1 = (s32[2,3,128]{2,0,1:T(2,128)S(1)}, s32[2,3,128]{2,0,1:T(2,128)S(1)}, u32[]{:S(2)}, u32[]{:S(2)}) collective-permute-start(s32[2,3,128]{2,0,1:T(2,128)S(1)} %bitcast.82), channel_id=1, source_target_pairs={{0,16},{16,0},{1,17},{17,1},{2,18},{18,2},{3,19},{19,3},{4,20},{20... | collective-permute-start | bytes 9224 | tf_op jit(solution)/shard_map/ppermute | solution.py:340
  27.1 15.4 %all-to-all-start = ((f32[4,56,256]{2,1,0:T(8,128)}), f32[4,56,256]{2,1,0:T(8,128)S(1)}, u32[]{:S(2)}, u32[]{:S(2)}) async-start(f32[4,56,256]{2,1,0:T(8,128)} %slice_rows.1), calls=%async_computation | async-start | bytes 458752 | tf_op jit(solution)/shard_map/all_to_all | solution.py:334
  47.2 4.6 %collective-permute-start.3 = (s32[2,4,3,128]{3,1,2,0:T(4,128)S(1)}, s32[2,4,3,128]{3,1,2,0:T(4,128)S(1)}, u32[]{:S(2)}, u32[]{:S(2)}) collective-permute-start(s32[2,4,3,128]{3,1,2,0:T(4,128)S(1)} %pad_add_fusion.2), channel_id=1, source_target_pairs={{0,3},{1,2},{2,1},{3,0},{4,7},{5,6},{6,5},{7,4},{8,11},{9,10},{10,... | collective-permute-start | bytes 36872 | tf_op jit(solution)/shard_map/ppermute | solution.py:339
  57.8 4.4 %collective-permute-start.5 = (s32[8,4,3,128]{3,1,2,0:T(4,128)S(1)}, s32[8,4,3,128]{3,1,2,0:T(4,128)S(1)}, u32[]{:S(2)}, u32[]{:S(2)}) collective-permute-start(s32[8,4,3,128]{3,1,2,0:T(4,128)S(1)} %pad_add_fusion), channel_id=1, source_target_pairs={{0,12},{4,8},{8,4},{12,0},{1,13},{5,9},{9,5},{13,1},{2,14},{6,10},... | collective-permute-start | bytes 147464 | tf_op jit(solution)/shard_map/ppermute | solution.py:339
  66.6 6.6 %collective-permute-start.9 = (f32[4,56,256]{2,1,0:T(8,128)S(1)}, f32[4,56,256]{2,1,0:T(8,128)S(1)}, u32[]{:S(2)}, u32[]{:S(2)}) collective-permute-start(f32[4,56,256]{2,1,0:T(8,128)S(1)} %all-to-all-done), channel_id=1, source_target_pairs={{0,64},{64,128},{128,192},{192,256},{256,320},{320,384},{384,448},... | collective-permute-start | bytes 688136 | tf_op jit(solution)/shard_map/ppermute | solution.py:382
  73.2 9.4 %collective-permute-start.6 = (f32[4,56,256]{2,1,0:T(8,128)S(1)}, f32[4,56,256]{2,1,0:T(8,128)S(1)}, u32[]{:S(2)}, u32[]{:S(2)}) collective-permute-start(f32[4,56,256]{2,1,0:T(8,128)S(1)} %all-to-all-done), channel_id=1, source_target_pairs={{0,960},{64,0},{128,64},{192,128},{256,192},{320,256},{384,320},{4... | collective-permute-start | bytes 688136 | tf_op jit(solution)/shard_map/ppermute | solution.py:382
  86.6 5.2 %collective-permute-start.8 = (f32[2,56,256]{2,1,0:T(8,128)S(1)}, f32[2,56,256]{2,1,0:T(8,128)S(1)}, u32[]{:S(2)}, u32[]{:S(2)}) collective-permute-start(f32[2,56,256]{2,1,0:T(8,128)S(1)} %get-tuple-element.47), channel_id=1, source_target_pairs={{0,128},{64,192},{128,256},{192,320},{256,384},{320,448},{384,512}... | collective-permute-start | bytes 344072 | tf_op jit(solution)/shard_map/ppermute | solution.py:382
  92.4 5.8 %count_slots.1 = (bf16[3,512,512]{2,1,0:T(8,128)(2,1)}, bf16[3,512,512]{2,1,0:T(8,128)(2,1)}) custom-call(s32[3,1,2048]{2,1,0:T(1,128)} %bitcast.79, s32[3,1,2048]{2,1,0:T(1,128)} %bitcast.80, f32[3,1,512]{2,1,0:T(1,128)} %compare_convert_fusion.live_ref), custom_call_target="tpu_custom_call" | custom-call | tf_op jit(solution)/shard_map/count_slots/pallas_call | solution.py:143
  100.2 6.3 %serve_rows.1 = f32[64,3,2,8,128]{4,3,2,1,0:T(8,128)} custom-call(s32[1]{0:T(128)} %bitcast.1.me_ref, s32[1]{0:T(128)} %bitcast.2.mid_ref, s32[64,3,8,16]{3,2,1,0:T(8,128)} %copy.66.ids_ref, f32[4,4,56,256]{3,2,1,0:T(8,128)} %pad_maximum_fusion.slab_ref), custom_call_target="tpu_custom_call" | custom-call | tf_op jit(solution)/shard_map/serve_rows/pallas_call | solution.py:115
  106.6 16.6 %all-to-all-start.1 = ((f32[64,3,2,8,128]{4,3,2,1,0:T(8,128)}), f32[64,3,2,8,128]{4,3,2,1,0:T(8,128)S(1)}, u32[]{:S(2)}, u32[]{:S(2)}) async-start(f32[64,3,2,8,128]{4,3,2,1,0:T(8,128)} %serve_rows.1), calls=%async_computation.1 | async-start | bytes 3145728 | tf_op jit(solution)/shard_map/all_to_all | solution.py:334
  127.3 18.0 %all-to-all-done.1.fetched_ref = f32[64,3,2,8,128]{4,3,2,1,0:T(8,128)S(1)} async-done(((f32[64,3,2,8,128]{4,3,2,1,0:T(8,128)}), f32[64,3,2,8,128]{4,3,2,1,0:T(8,128)S(1)}, u32[]{:S(2)}, u32[]{:S(2)}) %all-to-all-start.1) | async-done | bytes 1572896 | tf_op jit(solution)/shard_map/all_to_all | solution.py:334
  146.4 11.1 %tower.1 = (f32[64,3,8,256]{3,2,1,0:T(8,128)}, bf16[512,768]{1,0:T(8,128)(2,1)}, bf16[512,512]{1,0:T(8,128)(2,1)}, f32[8,128]{1,0:T(8,128)}) custom-call(f32[64,3,2,8,128]{4,3,2,1,0:T(8,128)} %copy-done.1, bf16[3,512,512]{2,1,0:T(8,128)(2,1)} %get-tuple-element.28.count_ref, bf16[3,512,512]{2,1,0:T(8,128)(2,1)} %get-tuple-element.29.turned_ref, ...), custom_call_target="tpu_custom_call" | custom-call | tf_op jit(solution)/shard_map/tower/pallas_call | solution.py:228
  157.5 10.5 %all-to-all-start.2 = ((f32[64,3,8,256]{3,2,1,0:T(8,128)}), f32[64,3,8,256]{3,2,1,0:T(8,128)S(1)}, u32[]{:S(2)}, u32[]{:S(2)}) async-start(f32[64,3,8,256]{3,2,1,0:T(8,128)} %get-tuple-element.34), calls=%async_computation.2 | async-start | bytes 3145728 | tf_op jit(solution)/shard_map/all_to_all | solution.py:334
  180.0 11.2 %collective-permute-done.11 = f32[16,56,128]{2,1,0:T(8,128)S(1)} collective-permute-done((f32[16,56,128]{2,1,0:T(8,128)S(1)}, f32[16,56,128]{2,1,0:T(8,128)S(1)}, u32[]{:S(2)}, u32[]{:S(2)}) %collective-permute-start.11) | collective-permute-done | bytes 458784 | tf_op jit(solution)/shard_map/ppermute | solution.py:340
  193.5 5.6 %collective-permute-done.12 = f32[8,56,128]{2,1,0:T(8,128)S(1)} collective-permute-done((f32[8,56,128]{2,1,0:T(8,128)S(1)}, f32[8,56,128]{2,1,0:T(8,128)S(1)}, u32[]{:S(2)}, u32[]{:S(2)}) %collective-permute-start.12) | collective-permute-done | bytes 229408 | tf_op jit(solution)/shard_map/ppermute | solution.py:340
  201.7 4.5 %collective-permute-done.13 = f32[4,56,128]{2,1,0:T(8,128)S(1)} collective-permute-done((f32[4,56,128]{2,1,0:T(8,128)S(1)}, f32[4,56,128]{2,1,0:T(8,128)S(1)}, u32[]{:S(2)}, u32[]{:S(2)}) %collective-permute-start.13) | collective-permute-done | bytes 114720 | tf_op jit(solution)/shard_map/ppermute | solution.py:339
  215.7 86.0 %collective-permute-done.15 = f32[1,56,128]{2,1,0:T(8,128)S(1)} collective-permute-done((f32[1,56,128]{2,1,0:T(8,128)S(1)}, f32[1,56,128]{2,1,0:T(8,128)S(1)}, u32[]{:S(2)}, u32[]{:S(2)}) %collective-permute-start.15) | collective-permute-done | bytes 28704 | tf_op jit(solution)/shard_map/ppermute | solution.py:340
  307.9 8.0 %collective-permute-start.17 = (f32[56,128]{1,0:T(8,128)S(1)}, f32[56,128]{1,0:T(8,128)S(1)}, u32[]{:S(2)}, u32[]{:S(2)}) collective-permute-start(f32[56,128]{1,0:T(8,128)S(1)} %add.107), channel_id=1, source_target_pairs={{0,128},{128,0},{1,129},{129,1},{2,130},{130,2},{3,131},{131,3},{4... | collective-permute-start | bytes 86024 | tf_op jit(solution)/shard_map/ppermute | solution.py:340
  317.5 12.0 %collective-permute-start.18 = (f32[56,128]{1,0:T(8,128)S(1)}, f32[56,128]{1,0:T(8,128)S(1)}, u32[]{:S(2)}, u32[]{:S(2)}) collective-permute-start(f32[56,128]{1,0:T(8,128)S(1)} %add.108), channel_id=1, source_target_pairs={{0,256},{256,0},{1,257},{257,1},{2,258},{258,2},{3,259},{259,3},{4... | collective-permute-start | bytes 86024 | tf_op jit(solution)/shard_map/ppermute | solution.py:340
  330.8 14.9 %collective-permute-start.19 = (f32[56,128]{1,0:T(8,128)S(1)}, f32[56,128]{1,0:T(8,128)S(1)}, u32[]{:S(2)}, u32[]{:S(2)}) collective-permute-start(f32[56,128]{1,0:T(8,128)S(1)} %add.109), channel_id=1, source_target_pairs={{0,768},{256,512},{512,256},{768,0},{1,769},{257,513},{513,257},{7... | collective-permute-start | bytes 86024 | tf_op jit(solution)/shard_map/ppermute | solution.py:389
  366.9 5.1 %collective-permute-done.23 = f32[8,56,128]{2,1,0:T(8,128)S(1)} collective-permute-done((f32[8,56,128]{2,1,0:T(8,128)S(1)}, f32[8,56,128]{2,1,0:T(8,128)S(1)}, u32[]{:S(2)}, u32[]{:S(2)}) %collective-permute-start.23) | collective-permute-done | bytes 229408 | tf_op jit(solution)/shard_map/ppermute | solution.py:340
  374.0 7.3 %collective-permute-done.24 = f32[16,56,128]{2,1,0:T(8,128)S(1)} collective-permute-done((f32[16,56,128]{2,1,0:T(8,128)S(1)}, f32[16,56,128]{2,1,0:T(8,128)S(1)}, u32[]{:S(2)}, u32[]{:S(2)}) %collective-permute-start.24) | collective-permute-done | bytes 458784 | tf_op jit(solution)/shard_map/ppermute | solution.py:340
  381.3 11.6 %collective-permute-start.25 = (f32[32,56,128]{2,1,0:T(8,128)S(1)}, f32[32,56,128]{2,1,0:T(8,128)S(1)}, u32[]{:S(2)}, u32[]{:S(2)}) collective-permute-start(f32[32,56,128]{2,1,0:T(8,128)S(1)} %constant_dynamic-update-slice_fusion.10.low_ref), channel_id=1, source_target_pairs={{0,16},{16,0},{1,17},{17,1},{2,18},{18,2},{3,19},{19,3},{4,20},{20... | collective-permute-start | bytes 2752520 | tf_op jit(solution)/shard_map/ppermute | solution.py:340
  (121 shorter events, 94.4 us)
Async XLA Ops:
  7.5 17.0 %collective-permute-start.1 = (s32[2,3,128]{2,0,1:T(2,128)S(1)}, s32[2,3,128]{2,0,1:T(2,128)S(1)}, u32[]{:S(2)}, u32[]{:S(2)}) collective-permute-start(s32[2,3,128]{2,0,1:T(2,128)S(1)} %bitcast.82), channel_id=1, source_target_pairs={{0,16},{16,0},{1,17},{17,1},{2,18},{18,2},{3,19},{19,3},{4,20},{20... | collective-permute-start | bytes 9224 | tf_op jit(solution)/shard_map/ppermute | solution.py:340
  27.1 39.5 %all-to-all-start = ((f32[4,56,256]{2,1,0:T(8,128)}), f32[4,56,256]{2,1,0:T(8,128)S(1)}, u32[]{:S(2)}, u32[]{:S(2)}) async-start(f32[4,56,256]{2,1,0:T(8,128)} %slice_rows.1), calls=%async_computation | async-start | bytes 458752 | tf_op jit(solution)/shard_map/all_to_all | solution.py:334
  47.2 6.0 %collective-permute-start.3 = (s32[2,4,3,128]{3,1,2,0:T(4,128)S(1)}, s32[2,4,3,128]{3,1,2,0:T(4,128)S(1)}, u32[]{:S(2)}, u32[]{:S(2)}) collective-permute-start(s32[2,4,3,128]{3,1,2,0:T(4,128)S(1)} %pad_add_fusion.2), channel_id=1, source_target_pairs={{0,3},{1,2},{2,1},{3,0},{4,7},{5,6},{6,5},{7,4},{8,11},{9,10},{10,... | collective-permute-start | bytes 36872 | tf_op jit(solution)/shard_map/ppermute | solution.py:339
  57.8 6.3 %collective-permute-start.5 = (s32[8,4,3,128]{3,1,2,0:T(4,128)S(1)}, s32[8,4,3,128]{3,1,2,0:T(4,128)S(1)}, u32[]{:S(2)}, u32[]{:S(2)}) collective-permute-start(s32[8,4,3,128]{3,1,2,0:T(4,128)S(1)} %pad_add_fusion), channel_id=1, source_target_pairs={{0,12},{4,8},{8,4},{12,0},{1,13},{5,9},{9,5},{13,1},{2,14},{6,10},... | collective-permute-start | bytes 147464 | tf_op jit(solution)/shard_map/ppermute | solution.py:339
  66.6 32.6 %collective-permute-start.9 = (f32[4,56,256]{2,1,0:T(8,128)S(1)}, f32[4,56,256]{2,1,0:T(8,128)S(1)}, u32[]{:S(2)}, u32[]{:S(2)}) collective-permute-start(f32[4,56,256]{2,1,0:T(8,128)S(1)} %all-to-all-done), channel_id=1, source_target_pairs={{0,64},{64,128},{128,192},{192,256},{256,320},{320,384},{384,448},... | collective-permute-start | bytes 688136 | tf_op jit(solution)/shard_map/ppermute | solution.py:382
  73.2 26.0 %collective-permute-start.6 = (f32[4,56,256]{2,1,0:T(8,128)S(1)}, f32[4,56,256]{2,1,0:T(8,128)S(1)}, u32[]{:S(2)}, u32[]{:S(2)}) collective-permute-start(f32[4,56,256]{2,1,0:T(8,128)S(1)} %all-to-all-done), channel_id=1, source_target_pairs={{0,960},{64,0},{128,64},{192,128},{256,192},{320,256},{384,320},{4... | collective-permute-start | bytes 688136 | tf_op jit(solution)/shard_map/ppermute | solution.py:382
  82.6 16.5 %collective-permute-start.7 = (f32[2,56,256]{2,1,0:T(8,128)S(1)}, f32[2,56,256]{2,1,0:T(8,128)S(1)}, u32[]{:S(2)}, u32[]{:S(2)}) collective-permute-start(f32[2,56,256]{2,1,0:T(8,128)S(1)} %get-tuple-element.46), channel_id=1, source_target_pairs={{0,896},{64,960},{128,0},{192,64},{256,128},{320,192},{384,256},{4... | collective-permute-start | bytes 344072 | tf_op jit(solution)/shard_map/ppermute | solution.py:382
  86.6 12.5 %collective-permute-start.8 = (f32[2,56,256]{2,1,0:T(8,128)S(1)}, f32[2,56,256]{2,1,0:T(8,128)S(1)}, u32[]{:S(2)}, u32[]{:S(2)}) collective-permute-start(f32[2,56,256]{2,1,0:T(8,128)S(1)} %get-tuple-element.47), channel_id=1, source_target_pairs={{0,128},{64,192},{128,256},{192,320},{256,384},{320,448},{384,512}... | collective-permute-start | bytes 344072 | tf_op jit(solution)/shard_map/ppermute | solution.py:382
  106.6 38.7 %all-to-all-start.1 = ((f32[64,3,2,8,128]{4,3,2,1,0:T(8,128)}), f32[64,3,2,8,128]{4,3,2,1,0:T(8,128)S(1)}, u32[]{:S(2)}, u32[]{:S(2)}) async-start(f32[64,3,2,8,128]{4,3,2,1,0:T(8,128)} %serve_rows.1), calls=%async_computation.1 | async-start | bytes 3145728 | tf_op jit(solution)/shard_map/all_to_all | solution.py:334
  157.5 235.4 %all-to-all-start.2 = ((f32[64,3,8,256]{3,2,1,0:T(8,128)}), f32[64,3,8,256]{3,2,1,0:T(8,128)S(1)}, u32[]{:S(2)}, u32[]{:S(2)}) async-start(f32[64,3,8,256]{3,2,1,0:T(8,128)} %get-tuple-element.34), calls=%async_computation.2 | async-start | bytes 3145728 | tf_op jit(solution)/shard_map/all_to_all | solution.py:334
  177.6 13.6 %collective-permute-start.11 = (f32[16,56,128]{2,1,0:T(8,128)S(1)}, f32[16,56,128]{2,1,0:T(8,128)S(1)}, u32[]{:S(2)}, u32[]{:S(2)}) collective-permute-start(f32[16,56,128]{2,1,0:T(8,128)S(1)} %slice.106), channel_id=1, source_target_pairs={{0,1},{1,0},{2,3},{3,2},{4,5},{5,4},{6,7},{7,6},{8,9},{9,8},{10,11... | collective-permute-start | bytes 1376264 | tf_op jit(solution)/shard_map/ppermute | solution.py:340
  191.3 7.8 %collective-permute-start.12 = (f32[8,56,128]{2,1,0:T(8,128)S(1)}, f32[8,56,128]{2,1,0:T(8,128)S(1)}, u32[]{:S(2)}, u32[]{:S(2)}) collective-permute-start(f32[8,56,128]{2,1,0:T(8,128)S(1)} %slice.108), channel_id=1, source_target_pairs={{0,4},{4,0},{1,5},{5,1},{2,6},{6,2},{3,7},{7,3},{8,12},{12,8},{9,1... | collective-permute-start | bytes 688136 | tf_op jit(solution)/shard_map/ppermute | solution.py:340
  199.1 7.0 %collective-permute-start.13 = (f32[4,56,128]{2,1,0:T(8,128)S(1)}, f32[4,56,128]{2,1,0:T(8,128)S(1)}, u32[]{:S(2)}, u32[]{:S(2)}) collective-permute-start(f32[4,56,128]{2,1,0:T(8,128)S(1)} %slice.110), channel_id=1, source_target_pairs={{0,3},{1,2},{2,1},{3,0},{4,7},{5,6},{6,5},{7,4},{8,11},{9,10},{10,... | collective-permute-start | bytes 344072 | tf_op jit(solution)/shard_map/ppermute | solution.py:339
  206.2 6.4 %collective-permute-start.14 = (f32[2,56,128]{2,1,0:T(8,128)S(1)}, f32[2,56,128]{2,1,0:T(8,128)S(1)}, u32[]{:S(2)}, u32[]{:S(2)}) collective-permute-start(f32[2,56,128]{2,1,0:T(8,128)S(1)} %slice.112), channel_id=1, source_target_pairs={{0,12},{4,8},{8,4},{12,0},{1,13},{5,9},{9,5},{13,1},{2,14},{6,10},... | collective-permute-start | bytes 172040 | tf_op jit(solution)/shard_map/ppermute | solution.py:339
  212.6 89.1 %collective-permute-start.15 = (f32[1,56,128]{2,1,0:T(8,128)S(1)}, f32[1,56,128]{2,1,0:T(8,128)S(1)}, u32[]{:S(2)}, u32[]{:S(2)}) collective-permute-start(f32[1,56,128]{2,1,0:T(8,128)S(1)} %slice.114), channel_id=1, source_target_pairs={{0,32},{32,0},{1,33},{33,1},{2,34},{34,2},{3,35},{35,3},{4,36},{36... | collective-permute-start | bytes 86024 | tf_op jit(solution)/shard_map/ppermute | solution.py:340
  301.7 6.2 %collective-permute-start.16 = (f32[56,128]{1,0:T(8,128)S(1)}, f32[56,128]{1,0:T(8,128)S(1)}, u32[]{:S(2)}, u32[]{:S(2)}) collective-permute-start(f32[56,128]{1,0:T(8,128)S(1)} %fusion.2), channel_id=1, source_target_pairs={{0,64},{64,0},{1,65},{65,1},{2,66},{66,2},{3,67},{67,3},{4,68},{68... | collective-permute-start | bytes 86024 | tf_op jit(solution)/shard_map/ppermute | solution.py:340
  307.9 9.5 %collective-permute-start.17 = (f32[56,128]{1,0:T(8,128)S(1)}, f32[56,128]{1,0:T(8,128)S(1)}, u32[]{:S(2)}, u32[]{:S(2)}) collective-permute-start(f32[56,128]{1,0:T(8,128)S(1)} %add.107), channel_id=1, source_target_pairs={{0,128},{128,0},{1,129},{129,1},{2,130},{130,2},{3,131},{131,3},{4... | collective-permute-start | bytes 86024 | tf_op jit(solution)/shard_map/ppermute | solution.py:340
  317.5 13.3 %collective-permute-start.18 = (f32[56,128]{1,0:T(8,128)S(1)}, f32[56,128]{1,0:T(8,128)S(1)}, u32[]{:S(2)}, u32[]{:S(2)}) collective-permute-start(f32[56,128]{1,0:T(8,128)S(1)} %add.108), channel_id=1, source_target_pairs={{0,256},{256,0},{1,257},{257,1},{2,258},{258,2},{3,259},{259,3},{4... | collective-permute-start | bytes 86024 | tf_op jit(solution)/shard_map/ppermute | solution.py:340
  330.8 16.3 %collective-permute-start.19 = (f32[56,128]{1,0:T(8,128)S(1)}, f32[56,128]{1,0:T(8,128)S(1)}, u32[]{:S(2)}, u32[]{:S(2)}) collective-permute-start(f32[56,128]{1,0:T(8,128)S(1)} %add.109), channel_id=1, source_target_pairs={{0,768},{256,512},{512,256},{768,0},{1,769},{257,513},{513,257},{7... | collective-permute-start | bytes 86024 | tf_op jit(solution)/shard_map/ppermute | solution.py:389
  352.1 6.1 %collective-permute-start.21 = (f32[2,56,128]{2,1,0:T(8,128)S(1)}, f32[2,56,128]{2,1,0:T(8,128)S(1)}, u32[]{:S(2)}, u32[]{:S(2)}) collective-permute-start(f32[2,56,128]{2,1,0:T(8,128)S(1)} %pad_maximum_fusion.4), channel_id=1, source_target_pairs={{0,12},{4,8},{8,4},{12,0},{1,13},{5,9},{9,5},{13,1},{2,14},{6,10},... | collective-permute-start | bytes 172040 | tf_op jit(solution)/shard_map/ppermute | solution.py:339
  358.2 6.7 %collective-permute-start.22 = (f32[4,56,128]{2,1,0:T(8,128)S(1)}, f32[4,56,128]{2,1,0:T(8,128)S(1)}, u32[]{:S(2)}, u32[]{:S(2)}) collective-permute-start(f32[4,56,128]{2,1,0:T(8,128)S(1)} %pad_maximum_fusion.3), channel_id=1, source_target_pairs={{0,3},{1,2},{2,1},{3,0},{4,7},{5,6},{6,5},{7,4},{8,11},{9,10},{10,... | collective-permute-start | bytes 344072 | tf_op jit(solution)/shard_map/ppermute | solution.py:339
  365.0 7.1 %collective-permute-start.23 = (f32[8,56,128]{2,1,0:T(8,128)S(1)}, f32[8,56,128]{2,1,0:T(8,128)S(1)}, u32[]{:S(2)}, u32[]{:S(2)}) collective-permute-start(f32[8,56,128]{2,1,0:T(8,128)S(1)} %pad_maximum_fusion.1), channel_id=1, source_target_pairs={{0,4},{4,0},{1,5},{5,1},{2,6},{6,2},{3,7},{7,3},{8,12},{12,8},{9,1... | collective-permute-start | bytes 688136 | tf_op jit(solution)/shard_map/ppermute | solution.py:340
  372.1 9.2 %collective-permute-start.24 = (f32[16,56,128]{2,1,0:T(8,128)S(1)}, f32[16,56,128]{2,1,0:T(8,128)S(1)}, u32[]{:S(2)}, u32[]{:S(2)}) collective-permute-start(f32[16,56,128]{2,1,0:T(8,128)S(1)} %get-tuple-element.44), channel_id=1, source_target_pairs={{0,1},{1,0},{2,3},{3,2},{4,5},{5,4},{6,7},{7,6},{8,9},{9,8},{10,11... | collective-permute-start | bytes 1376264 | tf_op jit(solution)/shard_map/ppermute | solution.py:340
  381.3 13.8 %collective-permute-start.25 = (f32[32,56,128]{2,1,0:T(8,128)S(1)}, f32[32,56,128]{2,1,0:T(8,128)S(1)}, u32[]{:S(2)}, u32[]{:S(2)}) collective-permute-start(f32[32,56,128]{2,1,0:T(8,128)S(1)} %constant_dynamic-update-slice_fusion.10.low_ref), channel_id=1, source_target_pairs={{0,16},{16,0},{1,17},{17,1},{2,18},{18,2},{3,19},{19,3},{4,20},{20... | collective-permute-start | bytes 2752520 | tf_op jit(solution)/shard_map/ppermute | solution.py:340
  (9 other events, 89.5 us)

commit v4 on v3

--- a/solution.py
+++ b/solution.py
@@ -42,7 +42,7 @@
 COLUMN = (*FAR, *MID, "near", "core")
 DP = ("x1", "x0", "y1", "y0")
 SERVERS = ("near", "core", *DP)
-SUMMERS = ("core", "y0", "x0", "y1", "x1", "near")
+SUMMERS = ("core", "y1", "y0", "x1", "x0", "near")
 CHUNK = 32
 VMEM = 56 * 1024 * 1024
 LESS_VMEM = 16 * 1024 * 1024
@@ -363,6 +363,13 @@
     return x
 
 
+def ring_gather(x, ring):
+    half = x.shape[0] // 2
+    one, other = partner(x, ring + "0"), partner(x, ring + "1")
+    opposite = [partner(other[:half], ring + "0"), partner(one[half:], ring + "1")]
+    return jnp.concatenate([x, one, other, *opposite])
+
+
 def relative(x, axes):
     shape = x.shape
     for at, axis in enumerate(axes):
@@ -436,7 +443,8 @@
     grad_shard = scatter_rows(asked, swap(back, COLUMN))
     me = pair_place(SUMMERS).reshape(1)
     piece = pair_scatter_sum(weight_pieces(me, features, grad_pre, extra), SUMMERS)
-    low = pair_gather(sum_over_z(piece)[None], SUMMERS[1:])
+    low = pair_gather(sum_over_z(piece)[None], ("near",))
+    low = ring_gather(ring_gather(low, "x"), "y")
     high, grad_shard = lax.optimization_barrier((partner(low, SUMMERS[0]), grad_shard))
     grad_w, grad_b, grad_out = unpack(me, low, high)
     return grad_shard[None], grad_w, grad_b.reshape(HIDDEN), grad_out.reshape(HIDDEN)

time: 398 us -> 400 us (level)
  starting transfers between devices: 181 us -> 191 us
  waiting for transfers between devices: 170 us -> 162 us
    ppermute x15 -> x17, waiting for transfers between devices: 130 us -> 111 us  [partner(): return lax.ppermute(x, axis, [(0, 1), (1, 0)])]
    ppermute x6 -> x8, waiting for transfers between devices: 18 us -> 29.6 us  [partner(): lax.ppermute(x, (axis, axis[0] + '0'), [(i, 3 - i) for i in range(4)])]
    ppermute x6 -> x8, starting transfers between devices: 20.5 us -> 26.7 us  [partner(): lax.ppermute(x, (axis, axis[0] + '0'), [(i, 3 - i) for i in range(4)])]
    ppermute x15 -> x17, starting transfers between devices: 78 us -> 82.1 us  [partner(): return lax.ppermute(x, axis, [(0, 1), (1, 0)])]
  transfers between devices with their start and end apart: 29 -> 33, of which waited for: 23 -> 24; matrix products, arithmetic and copies ran while one was open for 2% -> 2% of each run, Pallas kernels for 3% -> 3%
where the time goes in v4:
time: 400 us; the launch traced here: 399 us
  starting transfers between devices  191 us (48%)
  waiting for transfers between devices  162 us (40%)
  Pallas kernels  32.1 us (8%)
  local copies, waits for them, and re-layouts  9.85 us (2%)
    ppermute x17, waiting for transfers between devices, partner(): return lax.ppermute(x, axis, [(0, 1), (1, 0)])  111 us
    ppermute x17, starting transfers between devices, partner(): return lax.ppermute(x, axis, [(0, 1), (1, 0)])  82.1 us
    all_to_all x3, starting transfers between devices, swap(): return lax.all_to_all(x, axes, split_axis=0, concat_axis=0, tiled=True)  42.5 us
    ppermute x8, waiting for transfers between devices, partner(): lax.ppermute(x, (axis, axis[0] + '0'), [(i, 3 - i) for i in range(4)])  29.6 us
    ppermute x8, starting transfers between devices, partner(): lax.ppermute(x, (axis, axis[0] + '0'), [(i, 3 - i) for i in range(4)])  26.7 us
    ppermute x4, starting transfers between devices, shift(): return lax.ppermute(x, axes, [(i, (i + by) % count) for i in range(count)])  25.2 us
    all_to_all x3, waiting for transfers between devices, swap(): return lax.all_to_all(x, axes, split_axis=0, concat_axis=0, tiled=True)  20.2 us
    ppermute x1, starting transfers between devices, sum_over_z(): return x + lax.ppermute(x, FAR, [(i, N_FAR - 1 - i) for i in range(N_FAR)])  14.9 us
  transfers between devices with their start and end apart: 33, of which 24 were waited for; matrix products, arithmetic and copies ran while one was open for 2% of the time, Pallas kernels for 3%

profile of v4, /device:TPU:1, one launch (start us, length us, event | category | flops | bytes accessed | tf_op | source)
XLA Modules:
  0.0 399.0 jit_solution(4762882180550789172)
XLA Ops:
  2.1 4.4 %collective-permute-start = (s32[2,3,128]{2,0,1:T(2,128)S(1)}, s32[2,3,128]{2,0,1:T(2,128)S(1)}, u32[]{:S(2)}, u32[]{:S(2)}) collective-permute-start(s32[2,3,128]{2,0,1:T(2,128)S(1)} %get-tuple-element.61), channel_id=1, source_target_pairs={{0,32},{32,0},{1,33},{33,1},{2,34},{34,2},{3,35},{35,3},{4,36},{36... | collective-permute-start | bytes 9224 | tf_op jit(solution)/shard_map/ppermute | solution.py:340
  7.5 16.2 %collective-permute-start.1 = (s32[2,3,128]{2,0,1:T(2,128)S(1)}, s32[2,3,128]{2,0,1:T(2,128)S(1)}, u32[]{:S(2)}, u32[]{:S(2)}) collective-permute-start(s32[2,3,128]{2,0,1:T(2,128)S(1)} %bitcast.82), channel_id=1, source_target_pairs={{0,16},{16,0},{1,17},{17,1},{2,18},{18,2},{3,19},{19,3},{4,20},{20... | collective-permute-start | bytes 9224 | tf_op jit(solution)/shard_map/ppermute | solution.py:340
  27.1 15.4 %all-to-all-start = ((f32[4,56,256]{2,1,0:T(8,128)}), f32[4,56,256]{2,1,0:T(8,128)S(1)}, u32[]{:S(2)}, u32[]{:S(2)}) async-start(f32[4,56,256]{2,1,0:T(8,128)} %slice_rows.1), calls=%async_computation | async-start | bytes 458752 | tf_op jit(solution)/shard_map/all_to_all | solution.py:334
  47.2 4.6 %collective-permute-start.3 = (s32[2,4,3,128]{3,1,2,0:T(4,128)S(1)}, s32[2,4,3,128]{3,1,2,0:T(4,128)S(1)}, u32[]{:S(2)}, u32[]{:S(2)}) collective-permute-start(s32[2,4,3,128]{3,1,2,0:T(4,128)S(1)} %pad_add_fusion.2), channel_id=1, source_target_pairs={{0,3},{1,2},{2,1},{3,0},{4,7},{5,6},{6,5},{7,4},{8,11},{9,10},{10,... | collective-permute-start | bytes 36872 | tf_op jit(solution)/shard_map/ppermute | solution.py:339
  57.8 4.4 %collective-permute-start.5 = (s32[8,4,3,128]{3,1,2,0:T(4,128)S(1)}, s32[8,4,3,128]{3,1,2,0:T(4,128)S(1)}, u32[]{:S(2)}, u32[]{:S(2)}) collective-permute-start(s32[8,4,3,128]{3,1,2,0:T(4,128)S(1)} %pad_add_fusion), channel_id=1, source_target_pairs={{0,12},{4,8},{8,4},{12,0},{1,13},{5,9},{9,5},{13,1},{2,14},{6,10},... | collective-permute-start | bytes 147464 | tf_op jit(solution)/shard_map/ppermute | solution.py:339
  66.6 6.6 %collective-permute-start.9 = (f32[4,56,256]{2,1,0:T(8,128)S(1)}, f32[4,56,256]{2,1,0:T(8,128)S(1)}, u32[]{:S(2)}, u32[]{:S(2)}) collective-permute-start(f32[4,56,256]{2,1,0:T(8,128)S(1)} %all-to-all-done), channel_id=1, source_target_pairs={{0,64},{64,128},{128,192},{192,256},{256,320},{320,384},{384,448},... | collective-permute-start | bytes 688136 | tf_op jit(solution)/shard_map/ppermute | solution.py:389
  73.2 9.4 %collective-permute-start.6 = (f32[4,56,256]{2,1,0:T(8,128)S(1)}, f32[4,56,256]{2,1,0:T(8,128)S(1)}, u32[]{:S(2)}, u32[]{:S(2)}) collective-permute-start(f32[4,56,256]{2,1,0:T(8,128)S(1)} %all-to-all-done), channel_id=1, source_target_pairs={{0,960},{64,0},{128,64},{192,128},{256,192},{320,256},{384,320},{4... | collective-permute-start | bytes 688136 | tf_op jit(solution)/shard_map/ppermute | solution.py:389
  82.6 4.0 %collective-permute-start.7 = (f32[2,56,256]{2,1,0:T(8,128)S(1)}, f32[2,56,256]{2,1,0:T(8,128)S(1)}, u32[]{:S(2)}, u32[]{:S(2)}) collective-permute-start(f32[2,56,256]{2,1,0:T(8,128)S(1)} %get-tuple-element.44), channel_id=1, source_target_pairs={{0,896},{64,960},{128,0},{192,64},{256,128},{320,192},{384,256},{4... | collective-permute-start | bytes 344072 | tf_op jit(solution)/shard_map/ppermute | solution.py:389
  86.6 5.2 %collective-permute-start.8 = (f32[2,56,256]{2,1,0:T(8,128)S(1)}, f32[2,56,256]{2,1,0:T(8,128)S(1)}, u32[]{:S(2)}, u32[]{:S(2)}) collective-permute-start(f32[2,56,256]{2,1,0:T(8,128)S(1)} %get-tuple-element.45), channel_id=1, source_target_pairs={{0,128},{64,192},{128,256},{192,320},{256,384},{320,448},{384,512}... | collective-permute-start | bytes 344072 | tf_op jit(solution)/shard_map/ppermute | solution.py:389
  92.4 5.8 %count_slots.1 = (bf16[3,512,512]{2,1,0:T(8,128)(2,1)}, bf16[3,512,512]{2,1,0:T(8,128)(2,1)}) custom-call(s32[3,1,2048]{2,1,0:T(1,128)} %bitcast.79, s32[3,1,2048]{2,1,0:T(1,128)} %bitcast.80, f32[3,1,512]{2,1,0:T(1,128)} %compare_convert_fusion.live_ref), custom_call_target="tpu_custom_call" | custom-call | tf_op jit(solution)/shard_map/count_slots/pallas_call | solution.py:143
  100.3 6.3 %serve_rows.1 = f32[64,3,2,8,128]{4,3,2,1,0:T(8,128)} custom-call(s32[1]{0:T(128)} %bitcast.1.me_ref, s32[1]{0:T(128)} %bitcast.2.mid_ref, s32[64,3,8,16]{3,2,1,0:T(8,128)} %copy.66.ids_ref, f32[4,4,56,256]{3,2,1,0:T(8,128)} %pad_maximum_fusion.slab_ref), custom_call_target="tpu_custom_call" | custom-call | tf_op jit(solution)/shard_map/serve_rows/pallas_call | solution.py:115
  106.6 16.6 %all-to-all-start.1 = ((f32[64,3,2,8,128]{4,3,2,1,0:T(8,128)}), f32[64,3,2,8,128]{4,3,2,1,0:T(8,128)S(1)}, u32[]{:S(2)}, u32[]{:S(2)}) async-start(f32[64,3,2,8,128]{4,3,2,1,0:T(8,128)} %serve_rows.1), calls=%async_computation.1 | async-start | bytes 3145728 | tf_op jit(solution)/shard_map/all_to_all | solution.py:334
  127.3 18.0 %all-to-all-done.1.fetched_ref = f32[64,3,2,8,128]{4,3,2,1,0:T(8,128)S(1)} async-done(((f32[64,3,2,8,128]{4,3,2,1,0:T(8,128)}), f32[64,3,2,8,128]{4,3,2,1,0:T(8,128)S(1)}, u32[]{:S(2)}, u32[]{:S(2)}) %all-to-all-start.1) | async-done | bytes 1572896 | tf_op jit(solution)/shard_map/all_to_all | solution.py:334
  146.4 11.1 %tower.1 = (f32[64,3,8,256]{3,2,1,0:T(8,128)}, bf16[512,768]{1,0:T(8,128)(2,1)}, bf16[512,512]{1,0:T(8,128)(2,1)}, f32[8,128]{1,0:T(8,128)}) custom-call(f32[64,3,2,8,128]{4,3,2,1,0:T(8,128)} %copy-done.1, bf16[3,512,512]{2,1,0:T(8,128)(2,1)} %get-tuple-element.28.count_ref, bf16[3,512,512]{2,1,0:T(8,128)(2,1)} %get-tuple-element.29.turned_ref, ...), custom_call_target="tpu_custom_call" | custom-call | tf_op jit(solution)/shard_map/tower/pallas_call | solution.py:228
  157.5 10.5 %all-to-all-start.2 = ((f32[64,3,8,256]{3,2,1,0:T(8,128)}), f32[64,3,8,256]{3,2,1,0:T(8,128)S(1)}, u32[]{:S(2)}, u32[]{:S(2)}) async-start(f32[64,3,8,256]{3,2,1,0:T(8,128)} %get-tuple-element.34), calls=%async_computation.2 | async-start | bytes 3145728 | tf_op jit(solution)/shard_map/all_to_all | solution.py:334
  180.1 12.3 %collective-permute-done.11 = f32[16,56,128]{2,1,0:T(8,128)S(1)} collective-permute-done((f32[16,56,128]{2,1,0:T(8,128)S(1)}, f32[16,56,128]{2,1,0:T(8,128)S(1)}, u32[]{:S(2)}, u32[]{:S(2)}) %collective-permute-start.11) | collective-permute-done | bytes 458784 | tf_op jit(solution)/shard_map/ppermute | solution.py:339
  194.4 5.9 %collective-permute-done.12 = f32[8,56,128]{2,1,0:T(8,128)S(1)} collective-permute-done((f32[8,56,128]{2,1,0:T(8,128)S(1)}, f32[8,56,128]{2,1,0:T(8,128)S(1)}, u32[]{:S(2)}, u32[]{:S(2)}) %collective-permute-start.12) | collective-permute-done | bytes 229408 | tf_op jit(solution)/shard_map/ppermute | solution.py:340
  203.6 3.8 collective-permute-done.13
  215.7 86.0 %collective-permute-done.15 = f32[1,56,128]{2,1,0:T(8,128)S(1)} collective-permute-done((f32[1,56,128]{2,1,0:T(8,128)S(1)}, f32[1,56,128]{2,1,0:T(8,128)S(1)}, u32[]{:S(2)}, u32[]{:S(2)}) %collective-permute-start.15) | collective-permute-done | bytes 28704 | tf_op jit(solution)/shard_map/ppermute | solution.py:340
  308.0 8.0 %collective-permute-start.17 = (f32[56,128]{1,0:T(8,128)S(1)}, f32[56,128]{1,0:T(8,128)S(1)}, u32[]{:S(2)}, u32[]{:S(2)}) collective-permute-start(f32[56,128]{1,0:T(8,128)S(1)} %add.107), channel_id=1, source_target_pairs={{0,128},{128,0},{1,129},{129,1},{2,130},{130,2},{3,131},{131,3},{4... | collective-permute-start | bytes 86024 | tf_op jit(solution)/shard_map/ppermute | solution.py:340
  317.5 12.0 %collective-permute-start.18 = (f32[56,128]{1,0:T(8,128)S(1)}, f32[56,128]{1,0:T(8,128)S(1)}, u32[]{:S(2)}, u32[]{:S(2)}) collective-permute-start(f32[56,128]{1,0:T(8,128)S(1)} %add.108), channel_id=1, source_target_pairs={{0,256},{256,0},{1,257},{257,1},{2,258},{258,2},{3,259},{259,3},{4... | collective-permute-start | bytes 86024 | tf_op jit(solution)/shard_map/ppermute | solution.py:340
  330.8 14.9 %collective-permute-start.19 = (f32[56,128]{1,0:T(8,128)S(1)}, f32[56,128]{1,0:T(8,128)S(1)}, u32[]{:S(2)}, u32[]{:S(2)}) collective-permute-start(f32[56,128]{1,0:T(8,128)S(1)} %add.109), channel_id=1, source_target_pairs={{0,768},{256,512},{512,256},{768,0},{1,769},{257,513},{513,257},{7... | collective-permute-start | bytes 86024 | tf_op jit(solution)/shard_map/ppermute | solution.py:396
  371.0 3.4 collective-permute-done.26
  383.7 11.7 %collective-permute-start.29 = (f32[32,56,128]{2,1,0:T(8,128)S(1)}, f32[32,56,128]{2,1,0:T(8,128)S(1)}, u32[]{:S(2)}, u32[]{:S(2)}) collective-permute-start(f32[32,56,128]{2,1,0:T(8,128)S(1)} %constant_dynamic-update-slice_fusion.11.low_ref), channel_id=1, source_target_pairs={{0,16},{16,0},{1,17},{17,1},{2,18},{18,2},{3,19},{19,3},{4,20},{20... | collective-permute-start | bytes 2752520 | tf_op jit(solution)/shard_map/ppermute | solution.py:340
  (135 shorter events, 101.0 us)
Async XLA Ops:
  7.5 17.0 %collective-permute-start.1 = (s32[2,3,128]{2,0,1:T(2,128)S(1)}, s32[2,3,128]{2,0,1:T(2,128)S(1)}, u32[]{:S(2)}, u32[]{:S(2)}) collective-permute-start(s32[2,3,128]{2,0,1:T(2,128)S(1)} %bitcast.82), channel_id=1, source_target_pairs={{0,16},{16,0},{1,17},{17,1},{2,18},{18,2},{3,19},{19,3},{4,20},{20... | collective-permute-start | bytes 9224 | tf_op jit(solution)/shard_map/ppermute | solution.py:340
  27.1 39.5 %all-to-all-start = ((f32[4,56,256]{2,1,0:T(8,128)}), f32[4,56,256]{2,1,0:T(8,128)S(1)}, u32[]{:S(2)}, u32[]{:S(2)}) async-start(f32[4,56,256]{2,1,0:T(8,128)} %slice_rows.1), calls=%async_computation | async-start | bytes 458752 | tf_op jit(solution)/shard_map/all_to_all | solution.py:334
  47.2 6.0 %collective-permute-start.3 = (s32[2,4,3,128]{3,1,2,0:T(4,128)S(1)}, s32[2,4,3,128]{3,1,2,0:T(4,128)S(1)}, u32[]{:S(2)}, u32[]{:S(2)}) collective-permute-start(s32[2,4,3,128]{3,1,2,0:T(4,128)S(1)} %pad_add_fusion.2), channel_id=1, source_target_pairs={{0,3},{1,2},{2,1},{3,0},{4,7},{5,6},{6,5},{7,4},{8,11},{9,10},{10,... | collective-permute-start | bytes 36872 | tf_op jit(solution)/shard_map/ppermute | solution.py:339
  57.8 6.3 %collective-permute-start.5 = (s32[8,4,3,128]{3,1,2,0:T(4,128)S(1)}, s32[8,4,3,128]{3,1,2,0:T(4,128)S(1)}, u32[]{:S(2)}, u32[]{:S(2)}) collective-permute-start(s32[8,4,3,128]{3,1,2,0:T(4,128)S(1)} %pad_add_fusion), channel_id=1, source_target_pairs={{0,12},{4,8},{8,4},{12,0},{1,13},{5,9},{9,5},{13,1},{2,14},{6,10},... | collective-permute-start | bytes 147464 | tf_op jit(solution)/shard_map/ppermute | solution.py:339
  66.6 32.6 %collective-permute-start.9 = (f32[4,56,256]{2,1,0:T(8,128)S(1)}, f32[4,56,256]{2,1,0:T(8,128)S(1)}, u32[]{:S(2)}, u32[]{:S(2)}) collective-permute-start(f32[4,56,256]{2,1,0:T(8,128)S(1)} %all-to-all-done), channel_id=1, source_target_pairs={{0,64},{64,128},{128,192},{192,256},{256,320},{320,384},{384,448},... | collective-permute-start | bytes 688136 | tf_op jit(solution)/shard_map/ppermute | solution.py:389
  73.2 26.0 %collective-permute-start.6 = (f32[4,56,256]{2,1,0:T(8,128)S(1)}, f32[4,56,256]{2,1,0:T(8,128)S(1)}, u32[]{:S(2)}, u32[]{:S(2)}) collective-permute-start(f32[4,56,256]{2,1,0:T(8,128)S(1)} %all-to-all-done), channel_id=1, source_target_pairs={{0,960},{64,0},{128,64},{192,128},{256,192},{320,256},{384,320},{4... | collective-permute-start | bytes 688136 | tf_op jit(solution)/shard_map/ppermute | solution.py:389
  82.6 16.5 %collective-permute-start.7 = (f32[2,56,256]{2,1,0:T(8,128)S(1)}, f32[2,56,256]{2,1,0:T(8,128)S(1)}, u32[]{:S(2)}, u32[]{:S(2)}) collective-permute-start(f32[2,56,256]{2,1,0:T(8,128)S(1)} %get-tuple-element.44), channel_id=1, source_target_pairs={{0,896},{64,960},{128,0},{192,64},{256,128},{320,192},{384,256},{4... | collective-permute-start | bytes 344072 | tf_op jit(solution)/shard_map/ppermute | solution.py:389
  86.6 12.5 %collective-permute-start.8 = (f32[2,56,256]{2,1,0:T(8,128)S(1)}, f32[2,56,256]{2,1,0:T(8,128)S(1)}, u32[]{:S(2)}, u32[]{:S(2)}) collective-permute-start(f32[2,56,256]{2,1,0:T(8,128)S(1)} %get-tuple-element.45), channel_id=1, source_target_pairs={{0,128},{64,192},{128,256},{192,320},{256,384},{320,448},{384,512}... | collective-permute-start | bytes 344072 | tf_op jit(solution)/shard_map/ppermute | solution.py:389
  106.6 38.7 %all-to-all-start.1 = ((f32[64,3,2,8,128]{4,3,2,1,0:T(8,128)}), f32[64,3,2,8,128]{4,3,2,1,0:T(8,128)S(1)}, u32[]{:S(2)}, u32[]{:S(2)}) async-start(f32[64,3,2,8,128]{4,3,2,1,0:T(8,128)} %serve_rows.1), calls=%async_computation.1 | async-start | bytes 3145728 | tf_op jit(solution)/shard_map/all_to_all | solution.py:334
  157.5 237.9 %all-to-all-start.2 = ((f32[64,3,8,256]{3,2,1,0:T(8,128)}), f32[64,3,8,256]{3,2,1,0:T(8,128)S(1)}, u32[]{:S(2)}, u32[]{:S(2)}) async-start(f32[64,3,8,256]{3,2,1,0:T(8,128)} %get-tuple-element.34), calls=%async_computation.2 | async-start | bytes 3145728 | tf_op jit(solution)/shard_map/all_to_all | solution.py:334
  177.6 14.8 %collective-permute-start.11 = (f32[16,56,128]{2,1,0:T(8,128)S(1)}, f32[16,56,128]{2,1,0:T(8,128)S(1)}, u32[]{:S(2)}, u32[]{:S(2)}) collective-permute-start(f32[16,56,128]{2,1,0:T(8,128)S(1)} %slice.122), channel_id=1, source_target_pairs={{0,3},{1,2},{2,1},{3,0},{4,7},{5,6},{6,5},{7,4},{8,11},{9,10},{10,... | collective-permute-start | bytes 1376264 | tf_op jit(solution)/shard_map/ppermute | solution.py:339
  192.5 7.8 %collective-permute-start.12 = (f32[8,56,128]{2,1,0:T(8,128)S(1)}, f32[8,56,128]{2,1,0:T(8,128)S(1)}, u32[]{:S(2)}, u32[]{:S(2)}) collective-permute-start(f32[8,56,128]{2,1,0:T(8,128)S(1)} %slice.124), channel_id=1, source_target_pairs={{0,1},{1,0},{2,3},{3,2},{4,5},{5,4},{6,7},{7,6},{8,9},{9,8},{10,11... | collective-permute-start | bytes 688136 | tf_op jit(solution)/shard_map/ppermute | solution.py:340
  200.4 7.0 %collective-permute-start.13 = (f32[4,56,128]{2,1,0:T(8,128)S(1)}, f32[4,56,128]{2,1,0:T(8,128)S(1)}, u32[]{:S(2)}, u32[]{:S(2)}) collective-permute-start(f32[4,56,128]{2,1,0:T(8,128)S(1)} %slice.126), channel_id=1, source_target_pairs={{0,12},{4,8},{8,4},{12,0},{1,13},{5,9},{9,5},{13,1},{2,14},{6,10},... | collective-permute-start | bytes 344072 | tf_op jit(solution)/shard_map/ppermute | solution.py:339
  212.7 89.0 %collective-permute-start.15 = (f32[1,56,128]{2,1,0:T(8,128)S(1)}, f32[1,56,128]{2,1,0:T(8,128)S(1)}, u32[]{:S(2)}, u32[]{:S(2)}) collective-permute-start(f32[1,56,128]{2,1,0:T(8,128)S(1)} %slice.130), channel_id=1, source_target_pairs={{0,32},{32,0},{1,33},{33,1},{2,34},{34,2},{3,35},{35,3},{4,36},{36... | collective-permute-start | bytes 86024 | tf_op jit(solution)/shard_map/ppermute | solution.py:340
  301.7 6.2 %collective-permute-start.16 = (f32[56,128]{1,0:T(8,128)S(1)}, f32[56,128]{1,0:T(8,128)S(1)}, u32[]{:S(2)}, u32[]{:S(2)}) collective-permute-start(f32[56,128]{1,0:T(8,128)S(1)} %fusion.2), channel_id=1, source_target_pairs={{0,64},{64,0},{1,65},{65,1},{2,66},{66,2},{3,67},{67,3},{4,68},{68... | collective-permute-start | bytes 86024 | tf_op jit(solution)/shard_map/ppermute | solution.py:340
  308.0 9.5 %collective-permute-start.17 = (f32[56,128]{1,0:T(8,128)S(1)}, f32[56,128]{1,0:T(8,128)S(1)}, u32[]{:S(2)}, u32[]{:S(2)}) collective-permute-start(f32[56,128]{1,0:T(8,128)S(1)} %add.107), channel_id=1, source_target_pairs={{0,128},{128,0},{1,129},{129,1},{2,130},{130,2},{3,131},{131,3},{4... | collective-permute-start | bytes 86024 | tf_op jit(solution)/shard_map/ppermute | solution.py:340
  317.5 13.3 %collective-permute-start.18 = (f32[56,128]{1,0:T(8,128)S(1)}, f32[56,128]{1,0:T(8,128)S(1)}, u32[]{:S(2)}, u32[]{:S(2)}) collective-permute-start(f32[56,128]{1,0:T(8,128)S(1)} %add.108), channel_id=1, source_target_pairs={{0,256},{256,0},{1,257},{257,1},{2,258},{258,2},{3,259},{259,3},{4... | collective-permute-start | bytes 86024 | tf_op jit(solution)/shard_map/ppermute | solution.py:340
  330.8 16.3 %collective-permute-start.19 = (f32[56,128]{1,0:T(8,128)S(1)}, f32[56,128]{1,0:T(8,128)S(1)}, u32[]{:S(2)}, u32[]{:S(2)}) collective-permute-start(f32[56,128]{1,0:T(8,128)S(1)} %add.109), channel_id=1, source_target_pairs={{0,768},{256,512},{512,256},{768,0},{1,769},{257,513},{513,257},{7... | collective-permute-start | bytes 86024 | tf_op jit(solution)/shard_map/ppermute | solution.py:396
  352.1 6.1 %collective-permute-start.22 = (f32[2,56,128]{2,1,0:T(8,128)S(1)}, f32[2,56,128]{2,1,0:T(8,128)S(1)}, u32[]{:S(2)}, u32[]{:S(2)}) collective-permute-start(f32[2,56,128]{2,1,0:T(8,128)S(1)} %pad_maximum_fusion.2), channel_id=1, source_target_pairs={{0,12},{4,8},{8,4},{12,0},{1,13},{5,9},{9,5},{13,1},{2,14},{6,10},... | collective-permute-start | bytes 172040 | tf_op jit(solution)/shard_map/ppermute | solution.py:339
  366.5 8.0 %collective-permute-start.26 = (f32[8,56,128]{2,1,0:T(8,128)S(1)}, f32[8,56,128]{2,1,0:T(8,128)S(1)}, u32[]{:S(2)}, u32[]{:S(2)}) collective-permute-start(f32[8,56,128]{2,1,0:T(8,128)S(1)} %get-tuple-element.50), channel_id=1, source_target_pairs={{0,3},{1,2},{2,1},{3,0},{4,7},{5,6},{6,5},{7,4},{8,11},{9,10},{10,... | collective-permute-start | bytes 688136 | tf_op jit(solution)/shard_map/ppermute | solution.py:339
  368.6 7.8 %collective-permute-start.25 = (f32[8,56,128]{2,1,0:T(8,128)S(1)}, f32[8,56,128]{2,1,0:T(8,128)S(1)}, u32[]{:S(2)}, u32[]{:S(2)}) collective-permute-start(f32[8,56,128]{2,1,0:T(8,128)S(1)} %get-tuple-element.50), channel_id=1, source_target_pairs={{0,1},{1,0},{2,3},{3,2},{4,5},{5,4},{6,7},{7,6},{8,9},{9,8},{10,11... | collective-permute-start | bytes 688136 | tf_op jit(solution)/shard_map/ppermute | solution.py:340
  374.5 5.8 %collective-permute-start.27 = (f32[4,56,128]{2,1,0:T(8,128)S(1)}, f32[4,56,128]{2,1,0:T(8,128)S(1)}, u32[]{:S(2)}, u32[]{:S(2)}) collective-permute-start(f32[4,56,128]{2,1,0:T(8,128)S(1)} %slice.133), channel_id=1, source_target_pairs={{0,1},{1,0},{2,3},{3,2},{4,5},{5,4},{6,7},{7,6},{8,9},{9,8},{10,11... | collective-permute-start | bytes 344072 | tf_op jit(solution)/shard_map/ppermute | solution.py:340
  376.4 7.3 %collective-permute-start.28 = (f32[4,56,128]{2,1,0:T(8,128)S(1)}, f32[4,56,128]{2,1,0:T(8,128)S(1)}, u32[]{:S(2)}, u32[]{:S(2)}) collective-permute-start(f32[4,56,128]{2,1,0:T(8,128)S(1)} %slice.134), channel_id=1, source_target_pairs={{0,3},{1,2},{2,1},{3,0},{4,7},{5,6},{6,5},{7,4},{8,11},{9,10},{10,... | collective-permute-start | bytes 344072 | tf_op jit(solution)/shard_map/ppermute | solution.py:339
  383.7 13.8 %collective-permute-start.29 = (f32[32,56,128]{2,1,0:T(8,128)S(1)}, f32[32,56,128]{2,1,0:T(8,128)S(1)}, u32[]{:S(2)}, u32[]{:S(2)}) collective-permute-start(f32[32,56,128]{2,1,0:T(8,128)S(1)} %constant_dynamic-update-slice_fusion.11.low_ref), channel_id=1, source_target_pairs={{0,16},{16,0},{1,17},{17,1},{2,18},{18,2},{3,19},{19,3},{4,20},{20... | collective-permute-start | bytes 2752520 | tf_op jit(solution)/shard_map/ppermute | solution.py:340
  (13 other events, 111.6 us)
